TPU v7x, 256 devices: a whole 4x4x8 slice. The times are simulated.
256 devices in a mesh: slab: 64 (over z, x, core), chan: 4 (over y).
Axes of the slice: x: 4, y: 4, z: 8, core: 2. Of those that a mesh axis runs over, the one named last changes fastest.
Arguments:
- point_feats: bfloat16 [32, 65536], P(None, 'slab'), may hold values from -6 to 6
- cell_coords: int32 [3, 65536], P(None, 'slab'), may hold values from 0 to 2047, as said below
- send_counts: int32 [64, 64], P('slab'), may hold values from 1 to 16, as said below
- lift_weight: bfloat16 [32, 32], P(None, 'chan'), may hold values from -1 to 1
- spec_weight: float32 [2, 32, 32, 64, 64, 32], P(None, None, 'chan', 'slab'), may hold values from -3 to 3
- skip_weight: bfloat16 [32, 32], P(None, 'chan'), may hold values from -1 to 1
- spec_bias: float32 [32], P('chan'), may hold values from -3 to 3
- out_weight: bfloat16 [32, 4], P('chan'), may hold values from -1 to 1
- out_bias: float32 [4], replicated, may hold values from -4 to 4
Outputs:
- surface_fields: float32 [4, 65536], P(None, 'slab')
Inputs may be any that keep to these rules, and one draw needn't show every extreme that they name: `cell_coords`: the slot s * 1024 + d * 16 + j lies in slab d: its first coordinate // 32 equals d. `send_counts`: each entry counts the live slots of patch s for slab d; in every draw some slab receives 16 live points from every patch.
All inputs are finite; a program needn't handle non-finite values.
Results may differ from a plain program's by a relative error of at most 0.0013.
Values may be sent and summed in bfloat16 or wider, within the bound.
A program may use at most 192 MiB of HBM per device.

v0:
```python
import math

import jax
import jax.numpy as jnp
from jax import lax
from jax.sharding import PartitionSpec as P

GRID = 128
MZ = 32
SUB = 16


highest = lax.Precision.HIGHEST


def passed_along(value, axis, by):
    length = lax.axis_size(axis)
    pairs = [(i, i + by) for i in range(length) if 0 <= i + by < length]
    return lax.ppermute(value, axis, pairs)


def kept_modes():
    return jnp.concatenate([jnp.arange(MZ), jnp.arange(GRID - MZ, GRID)])


def tables(freqs, positions):
    product = freqs[:, None] * positions[None, :] % GRID
    angle = product.astype(jnp.float32) * (2.0 * math.pi / GRID)
    return (jnp.cos(angle), jnp.sin(angle))


def hat_table(start, frac, count):
    rows = lax.broadcasted_iota(jnp.int32, (count, start.shape[0]), 0)
    lower = jnp.where(rows == start[None, :], 1.0 - frac[None, :], 0.0)
    upper = jnp.where(rows == start[None, :] + 1, frac[None, :], 0.0)
    return lower + upper


def blocked(table, nblocks, width):
    return jnp.transpose(table.reshape(table.shape[0], nblocks, width), (1, 0, 2))


def forward_x(planes_data, cos_x, sin_x):
    real_part = planes_data[..., :MZ]
    imag_part = planes_data[..., MZ:]
    out_real = jnp.einsum("px,cxqk->qcpk", cos_x, real_part, precision=highest) + jnp.einsum(
        "px,cxqk->qcpk", sin_x, imag_part, precision=highest
    )
    out_imag = jnp.einsum("px,cxqk->qcpk", cos_x, imag_part, precision=highest) - jnp.einsum(
        "px,cxqk->qcpk", sin_x, real_part, precision=highest
    )
    return jnp.concatenate([out_real, out_imag], axis=-1)


def inverse_x(modes_data, cos_x, sin_x):
    real_part = modes_data[..., :MZ]
    imag_part = modes_data[..., MZ:]
    out_real = jnp.einsum("px,qcpk->cxqk", cos_x, real_part, precision=highest) - jnp.einsum(
        "px,qcpk->cxqk", sin_x, imag_part, precision=highest
    )
    out_imag = jnp.einsum("px,qcpk->cxqk", cos_x, imag_part, precision=highest) + jnp.einsum(
        "px,qcpk->cxqk", sin_x, real_part, precision=highest
    )
    return jnp.concatenate([out_real, out_imag], axis=-1)


def local(
    point_feats,
    cell_coords,
    send_counts,
    lift_weight,
    spec_weight,
    skip_weight,
    spec_bias,
    out_weight,
    out_bias,
):
    slabs = lax.axis_size("slab")
    points = point_feats.shape[1]
    capacity = points // slabs
    planes = GRID // slabs
    group = lift_weight.shape[1]
    nout = out_weight.shape[1]
    width = min(512, points)
    nblocks = points // width
    live = (
        lax.broadcasted_iota(jnp.int32, (slabs, capacity), 1) < send_counts[0][:, None]
    ).reshape(points)
    embed = jnp.dot(lift_weight.T, point_feats, preferred_element_type=jnp.float32)
    embed = jnp.where(live[None], embed, 0.0).astype(jnp.bfloat16)
    got_embed, got_coords = (
        lax.all_to_all(
            embed.reshape(group, slabs, capacity), "slab", split_axis=1, concat_axis=1, tiled=True
        ),
        lax.all_to_all(
            cell_coords.reshape(3, slabs, capacity), "slab", split_axis=1, concat_axis=1, tiled=True
        ),
    )
    got_embed = got_embed.reshape(group, points)
    got_coords = got_coords.reshape(3, points)
    cells = got_coords // SUB
    frac = ((got_coords % SUB).astype(jnp.float32) + 0.5) / SUB
    x_table = blocked(hat_table(cells[0] % planes, frac[0], planes + 1), nblocks, width)
    y_table = blocked(hat_table(cells[1], frac[1], GRID), nblocks, width)
    z_table = blocked(hat_table(cells[2], frac[2], GRID), nblocks, width)
    embed_blocks = blocked(got_embed, nblocks, width)

    def deposit(total, block):
        embed_block, x_block, y_block, z_block = block
        scaled = embed_block.astype(jnp.float32)[:, None, :] * x_block[None]
        spread = (scaled[:, :, None, :] * y_block[None, None]).reshape(-1, width)
        return (total + jnp.einsum("ab,zb->az", spread, z_block, precision=highest), None)

    accum, _ = lax.scan(
        deposit,
        jnp.zeros((group * (planes + 1) * GRID, GRID), jnp.float32),
        (embed_blocks, x_table, y_table, z_table),
    )
    accum = accum.reshape(group, planes + 1, GRID, GRID)
    incoming = passed_along(accum[:, planes:], "slab", 1)
    latent = jnp.concatenate([accum[:, :1] + incoming, accum[:, 1:planes]], axis=1).astype(
        jnp.bfloat16
    )
    modes = kept_modes()
    cos_z, sin_z = tables(jnp.arange(MZ, dtype=jnp.int32), jnp.arange(GRID, dtype=jnp.int32))
    cos_y, sin_y = tables(modes, jnp.arange(GRID, dtype=jnp.int32))
    forward_z = jnp.concatenate([cos_z, -sin_z], axis=0)
    zeroed = jnp.einsum("cxyz,kz->cxyk", latent.astype(jnp.float32), forward_z, precision=highest)
    a_real = zeroed[..., :MZ]
    a_imag = zeroed[..., MZ:]
    b_real = jnp.einsum("qy,cxyk->cxqk", cos_y, a_real, precision=highest) + jnp.einsum(
        "qy,cxyk->cxqk", sin_y, a_imag, precision=highest
    )
    b_imag = jnp.einsum("qy,cxyk->cxqk", cos_y, a_imag, precision=highest) - jnp.einsum(
        "qy,cxyk->cxqk", sin_y, a_real, precision=highest
    )
    partly = jnp.concatenate([b_real, b_imag], axis=-1)
    cos_all, sin_all = tables(modes, jnp.arange(GRID, dtype=jnp.int32))
    pencil = lax.all_to_all(partly, "slab", split_axis=2, concat_axis=1, tiled=True)
    spectra = forward_x(pencil, cos_all, sin_all)
    piece = lax.all_gather(spectra, "chan", axis=1, tiled=True)
    count = piece.shape[1]
    rows = piece.shape[0]
    firsts = piece.shape[2]
    span = firsts * MZ
    wpart = spec_weight
    outs_here = wpart.shape[2]
    w_flat = wpart.reshape(2, count, outs_here, rows, span)
    p_real = jnp.transpose(piece[..., :MZ].reshape(rows, count, span), (1, 0, 2))[:, None]
    p_imag = jnp.transpose(piece[..., MZ:].reshape(rows, count, span), (1, 0, 2))[:, None]
    d_real = jnp.sum(w_flat[0] * p_real - w_flat[1] * p_imag, axis=0)
    d_imag = jnp.sum(w_flat[0] * p_imag + w_flat[1] * p_real, axis=0)
    d_real = jnp.transpose(d_real, (1, 0, 2)).reshape(rows, outs_here, firsts, MZ)
    d_imag = jnp.transpose(d_imag, (1, 0, 2)).reshape(rows, outs_here, firsts, MZ)
    mixed = jnp.concatenate([d_real, d_imag], axis=-1)
    inverted = inverse_x(mixed, cos_all, sin_all)
    unfolded = lax.all_to_all(inverted, "slab", split_axis=1, concat_axis=2, tiled=True)
    e_real = unfolded[..., :MZ]
    e_imag = unfolded[..., MZ:]
    f_real = jnp.einsum("qy,cxqk->cxyk", cos_y, e_real, precision=highest) - jnp.einsum(
        "qy,cxqk->cxyk", sin_y, e_imag, precision=highest
    )
    f_imag = jnp.einsum("qy,cxqk->cxyk", cos_y, e_imag, precision=highest) + jnp.einsum(
        "qy,cxqk->cxyk", sin_y, e_real, precision=highest
    )
    factor = (
        jnp.where(jnp.arange(MZ) == 0, 1.0, 2.0).astype(jnp.float32)[:, None] / float(GRID) ** 3
    )
    spectral = jnp.einsum("cxyk,kz->cxyz", f_real, factor * cos_z, precision=highest) - jnp.einsum(
        "cxyk,kz->cxyz", f_imag, factor * sin_z, precision=highest
    )
    wpart = skip_weight
    skipped = jnp.einsum(
        "io,ixyz->oxyz",
        wpart,
        lax.all_gather(latent, "chan", axis=0, tiled=True),
        preferred_element_type=jnp.float32,
    )
    hidden = jax.nn.gelu(spectral + skipped + spec_bias[:, None, None, None]).astype(jnp.bfloat16)
    following = passed_along(hidden[:, :1], "slab", -1)
    extended = jnp.concatenate([hidden, following], axis=1).astype(jnp.float32)

    def sample(carry, block):
        x_block, y_block, z_block = block
        along_z = jnp.einsum("cxyz,zb->cxyb", extended, z_block, precision=highest)
        along_y = jnp.sum(along_z * y_block[None, None], axis=2)
        return (carry, jnp.sum(along_y * x_block[None], axis=1))

    _, sampled = lax.scan(sample, jnp.zeros((), jnp.float32), (x_table, y_table, z_table))
    samples = jnp.transpose(sampled, (1, 0, 2)).reshape(group, points)
    partial_heads = jnp.dot(out_weight.T.astype(jnp.float32), samples, precision=highest)
    heads = lax.psum(partial_heads, "chan")
    returned = lax.all_to_all(
        heads.reshape(nout, slabs, capacity), "slab", split_axis=1, concat_axis=1, tiled=True
    ).reshape(nout, points)
    return jnp.where(live[None], returned + out_bias[:, None], 0.0)


def solution(mesh):
    in_specs = (
        P(None, "slab"),
        P(None, "slab"),
        P("slab", None),
        P(None, "chan"),
        P(None, None, "chan", "slab", None, None),
        P(None, "chan"),
        P("chan"),
        P("chan", None),
        P(),
    )
    out_specs = P(None, "slab")
    return jax.shard_map(local, mesh=mesh, in_specs=in_specs, out_specs=out_specs, check_vma=False)
```

profile of v0, /device:TPU:1, one launch (start us, length us, event | category | flops | bytes accessed | tf_op | source)
XLA Modules:
  0.0 231.4 jit_solution(5251728972944701283)
XLA Ops:
  6.5 0.8 reshape.207
  7.4 0.7 copy.56
  8.1 13.0 %all-to-all-start = ((s32[3,64,16]{2,0,1:T(4,128)}), s32[3,64,16]{2,0,1:T(4,128)S(1)}, u32[]{:S(2)}, u32[]{:S(2)}) async-start(s32[3,64,16]{2,0,1:T(4,128)} %copy.56), calls=%async_computation | async-start | bytes 262144 | tf_op jit(solution)/shard_map/all_to_all | solution.py:95
  21.1 0.7 iota_compare_fusion.4
  21.9 0.8 fusion.19
  22.9 0.7 copy.58
  23.6 8.6 %all-to-all-done = s32[3,64,16]{2,0,1:T(4,128)S(1)} async-done(((s32[3,64,16]{2,0,1:T(4,128)}), s32[3,64,16]{2,0,1:T(4,128)S(1)}, u32[]{:S(2)}, u32[]{:S(2)}) %all-to-all-start) | async-done | bytes 12320 | tf_op jit(solution)/shard_map/all_to_all | solution.py:95
  32.2 4.4 %all-to-all-start.1 = ((bf16[8,64,16]{2,0,1:T(8,128)(2,1)}), bf16[8,64,16]{2,0,1:T(8,128)(2,1)S(1)}, u32[]{:S(2)}, u32[]{:S(2)}) async-start(bf16[8,64,16]{2,0,1:T(8,128)(2,1)} %copy.58), calls=%async_computation.1 | async-start | bytes 262144 | tf_op jit(solution)/shard_map/all_to_all | solution.py:92
  37.6 0.6 fusion.190
  38.4 9.6 %all-to-all-done.1 = bf16[8,64,16]{2,0,1:T(8,128)(2,1)S(1)} async-done(((bf16[8,64,16]{2,0,1:T(8,128)(2,1)}), bf16[8,64,16]{2,0,1:T(8,128)(2,1)S(1)}, u32[]{:S(2)}, u32[]{:S(2)}) %all-to-all-start.1) | async-done | bytes 16416 | tf_op jit(solution)/shard_map/all_to_all | solution.py:92
  48.2 21.5 %while.22 = (s32[]{:T(128)}, f32[3072,128]{1,0:T(8,128)S(1)}, bf16[2,8,512]{2,1,0:T(8,128)(2,1)S(1)}, f32[2,3,512]{2,1,0:T(4,128)S(1)}, f32[2,128,512]{2,1,0:T(8...) while((s32[]{:T(128)}, f32[3072,128]{1,0:T(8,128)S(1)}, ...), condition=%wide.region_1.2_spmd.clone, body=%wide.region_0.1_spmd.clone.sunk | while | flops 2418294784 | bytes 16935024 | solution.py:114
  48.3 3.5 %broadcast_multiply_fusion.5 = f32[8,3,128,512]{3,2,1,0:T(8,128)} fusion(f32[128,512]{1,0:T(8,128)S(1)} %dynamic-slice_bitcast_fusion.10, f32[8,3,512]{2,1,0:T(4,128)S(1)} %broadcast_multiply_fusion.4), kind=kLoop, calls=%fused_computation.10.clone.1 | loop fusion | flops 1572864 | bytes 6602752 | tf_op jit(solution)/shard_map/while/body/eval_jaxpr/mul | solution.py:111
  51.8 7.1 %convolution_add_fusion.6 = f32[3072,128]{1,0:T(8,128)S(1)} fusion(f32[3072,512]{1,0:T(8,128)} %bitcast.186, f32[3072,128]{1,0:T(8,128)S(1)} %get-tuple-element.246, pred[]{:T(512)S(6)} %compare.9, f32[2,128,512]{2,1,0:T(8,128)S(1)} %get-tuple-element.258, s32[]{:T(128)} %get-tuple-element.245), kind=kOutput, calls=%fused_computation.9.clone.1 | convolution fusion | flops 2416705536 | bytes 9699333 | tf_op jit(solution)/shard_map/while/body/eval_jaxpr/ab,zb->az/dot_general | solution.py:112
  59.0 3.5 %broadcast_multiply_fusion.5 = f32[8,3,128,512]{3,2,1,0:T(8,128)} fusion(f32[128,512]{1,0:T(8,128)S(1)} %dynamic-slice_bitcast_fusion.10, f32[8,3,512]{2,1,0:T(4,128)S(1)} %broadcast_multiply_fusion.4), kind=kLoop, calls=%fused_computation.10.clone.1 | loop fusion | flops 1572864 | bytes 6602752 | tf_op jit(solution)/shard_map/while/body/eval_jaxpr/mul | solution.py:111
  62.5 7.1 %convolution_add_fusion.6 = f32[3072,128]{1,0:T(8,128)S(1)} fusion(f32[3072,512]{1,0:T(8,128)} %bitcast.186, f32[3072,128]{1,0:T(8,128)S(1)} %get-tuple-element.246, pred[]{:T(512)S(6)} %compare.9, f32[2,128,512]{2,1,0:T(8,128)S(1)} %get-tuple-element.258, s32[]{:T(128)} %get-tuple-element.245), kind=kOutput, calls=%fused_computation.9.clone.1 | convolution fusion | flops 2416705536 | bytes 9699333 | tf_op jit(solution)/shard_map/while/body/eval_jaxpr/ab,zb->az/dot_general | solution.py:112
  69.7 2.2 collective-permute-start
  72.2 5.9 %collective-permute-done = f32[8,1,128,128]{3,2,1,0:T(8,128)S(1)} collective-permute-done((f32[8,1,128,128]{3,2,1,0:T(8,128)S(1)}, f32[8,1,128,128]{3,2,1,0:T(8,128)S(1)}, u32[]{:S(2)}, u32[]{:S(2)}) %collective-permute-start) | collective-permute-done | bytes 524320 | tf_op jit(solution)/shard_map/ppermute | solution.py:19
  78.1 0.7 fusion.50
  78.8 0.6 fusion.39
  79.3 0.6 fusion.35
  79.9 0.6 fusion.14
  80.4 0.6 fusion.13
  81.5 1.3 reshape.293
  82.8 8.7 %all-to-all-start.2 = ((f32[64,1,1024]{2,1,0:T(1,128)}), f32[64,1,1024]{2,1,0:T(1,128)S(1)}, u32[]{:S(2)}, u32[]{:S(2)}) async-start(f32[64,1,1024]{2,1,0:T(1,128)} %reshape.293), calls=%async_computation.2 | async-start | bytes 524288 | tf_op jit(solution)/shard_map/all_to_all | solution.py:139
  91.7 0.8 pad_maximum_fusion
  92.6 12.1 %all-to-all-done.2 = f32[64,1,1024]{2,1,0:T(1,128)S(1)} async-done(((f32[64,1,1024]{2,1,0:T(1,128)}), f32[64,1,1024]{2,1,0:T(1,128)S(1)}, u32[]{:S(2)}, u32[]{:S(2)}) %all-to-all-start.2) | async-done | bytes 262176 | tf_op jit(solution)/shard_map/all_to_all | solution.py:139
  105.1 1.2 reduce.53
  109.4 21.8 %all_gather.6 = f32[1,32,64,64]{3,2,0,1:T(8,128)S(1)} all-gather(f32[1,8,64,64]{3,2,0,1:T(8,128)S(1)} %copy.65), channel_id=1, replica_groups=mesh['slab'=64,'chan'=4] {'chan'}, dimensions={1}, use_global_device_ids=true | all-gather | bytes 655360 | tf_op jit(solution)/shard_map/all_gather | solution.py:141
  131.6 1.1 copy.66
  133.0 5.2 %subtract_reduce_fusion = (f32[8,64,32]{1,2,0:T(8,128)S(1)}, f32[8,64,32]{1,2,0:T(8,128)S(1)}) fusion(f32[2,32,8,1,64,32]{4,5,3,2,1,0:T(8,128)} %param.17, f32[32,64,32]{1,2,0:T(8,128)S(1)} %copy.67, f32[32,64,32]{1,2,0:T(8,128)} %copy.66), kind=kLoop, calls=%fused_computation.19 | loop fusion | flops 4161536 | bytes 4849664 | tf_op jit(solution)/shard_map/reduce_sum | solution.py:151
  140.3 1.0 reshape.295
  141.4 5.2 %all-to-all-start.3 = ((f32[64,1,1024]{2,1,0:T(1,128)}), f32[64,1,1024]{2,1,0:T(1,128)S(1)}, u32[]{:S(2)}, u32[]{:S(2)}) async-start(f32[64,1,1024]{2,1,0:T(1,128)} %reshape.295), calls=%async_computation.3 | async-start | bytes 524288 | tf_op jit(solution)/shard_map/all_to_all | solution.py:157
  146.6 13.1 %all-to-all-done.3 = f32[64,1,1024]{2,1,0:T(1,128)S(1)} async-done(((f32[64,1,1024]{2,1,0:T(1,128)}), f32[64,1,1024]{2,1,0:T(1,128)S(1)}, u32[]{:S(2)}, u32[]{:S(2)}) %all-to-all-start.3) | async-done | bytes 262176 | tf_op jit(solution)/shard_map/all_to_all | solution.py:157
  159.7 1.2 reduce.54
  161.3 0.6 fusion.29
  162.4 0.6 fusion.11
  163.0 0.6 fusion.12
  163.6 1.8 fusion.81
  165.4 2.8 %fusion.7 = f32[2,128,128,8]{2,3,1,0:T(8,128)S(1)} fusion(bf16[32,2,128,128]{3,2,1,0:T(8,128)(2,1)} %all-gather.2.cloned.1.call-done, bf16[32,8]{0,1:T(8,128)(2,1)S(1)} %copy-done.1), kind=kOutput, calls=%fused_computation.20 | convolution fusion | flops 16777216 | bytes 3146240 | tf_op jit(solution)/shard_map/io,ixyz->oxyz/dot_general | solution.py:173
  168.3 2.4 %fusion.27 = bf16[8,2,128,128]{3,2,1,0:T(8,128)(2,1)S(1)} fusion(f32[8,2,128,128]{3,2,1,0:T(8,128)S(1)} %fusion.81, f32[8,2,128,32]{2,3,1,0:T(8,128)S(1)} %fusion.11, f32[2,128,128,8]{2,3,1,0:T(8,128)S(1)} %fusion.7, f32[8]{0:T(128)S(1)} %copy-done.4, f32[32]{0:T(128)S(1)} %fusion.116), kind=kOutput, calls=%fused_computation.52 | convolution fusion | flops 103870464 | bytes 2883744 | tf_op jit(solution)/shard_map/cxyk,kz->cxyz/dot_general | solution.py:169
  170.6 2.2 collective-permute-start.1
  172.8 5.5 %collective-permute-done.1 = bf16[8,1,128,128]{3,2,1,0:T(8,128)(2,1)S(1)} collective-permute-done((bf16[8,1,128,128]{3,2,1,0:T(8,128)(2,1)S(1)}, bf16[8,1,128,128]{3,2,1,0:T(8,128)(2,1)S(1)}, u32[]{:S(2)}, u32[]{:S(2)}) %collective-permute-start.1) | collective-permute-done | bytes 262176 | tf_op jit(solution)/shard_map/ppermute | solution.py:19
  178.5 11.5 %while.21 = (s32[]{:T(128)}, f32[2,8,512]{2,1,0:T(8,128)S(1)}, f32[2,128,512]{2,1,0:T(8,128)S(1)}, f32[8,3,128,128]{3,2,1,0:T(8,128)S(1)}, f32[2,128,512]{2,1,0:...) while((s32[]{:T(128)}, f32[2,8,512]{2,1,0:T(8,128)S(1)}, f32[2,128,512]{2,1,0:T(8,128)S(1)}, ...), condition=%wide.region_7.8_spmd, body=%wide.region_4.7_spmd.sunk | while | flops 2419073024 | bytes 2787421 | solution.py:189
  178.5 5.6 %fusion.211 = f32[8,3,512]{2,1,0:T(4,128)S(1)} fusion(f32[128,512]{1,0:T(8,128)S(1)} %dynamic-slice_bitcast_fusion.8, f32[8,3,128,128]{3,2,1,0:T(8,128)S(1)} %get-tuple-element.278, f32[2,128,512]{2,1,0:T(8,128)S(1)} %get-tuple-element.277, s32[]{:T(128)} %get-tuple-element.268), kind=kOutput, calls=%fused_computation.1.clone.1 | convolution fusion | flops 2419052544 | bytes 2146308 | tf_op jit(solution)/shard_map/while/body/eval_jaxpr/cxyz,zb->cxyb/dot_general | solution.py:185
  184.3 5.6 %fusion.211 = f32[8,3,512]{2,1,0:T(4,128)S(1)} fusion(f32[128,512]{1,0:T(8,128)S(1)} %dynamic-slice_bitcast_fusion.8, f32[8,3,128,128]{3,2,1,0:T(8,128)S(1)} %get-tuple-element.278, f32[2,128,512]{2,1,0:T(8,128)S(1)} %get-tuple-element.277, s32[]{:T(128)} %get-tuple-element.268), kind=kOutput, calls=%fused_computation.1.clone.1 | convolution fusion | flops 2419052544 | bytes 2146308 | tf_op jit(solution)/shard_map/while/body/eval_jaxpr/cxyz,zb->cxyb/dot_general | solution.py:185
  190.2 14.4 %psum.7 = f32[4,64,16]{2,1,0:T(8,128)S(1)} all-reduce(f32[4,64,16]{2,1,0:T(8,128)S(1)} %reshape.214), channel_id=1, replica_groups=mesh['slab'=64,'chan'=4] {'chan'}, use_global_device_ids=true, to_apply=%region_8.9 | all-reduce | flops 4096 | bytes 32768 | tf_op jit(solution)/shard_map/psum | solution.py:192
  204.7 19.0 %all_to_all.51 = f32[4,64,16]{2,0,1:T(4,128)S(1)} all-to-all(f32[4,64,16]{2,0,1:T(4,128)S(1)} %copy.72), channel_id=1, replica_groups=mesh['slab'=64,'chan'=4] {'slab'}, dimensions={1} | all-to-all | bytes 32768 | tf_op jit(solution)/shard_map/all_to_all | solution.py:193
  223.9 0.7 add_select_fusion.4
  (98 shorter events, 10.7 us)
Async XLA Ops:
  6.5 15.4 %copy-start = (bf16[32,1024]{1,0:T(8,128)(2,1)S(1)}, bf16[32,1024]{1,0:T(8,128)(2,1)}, u32[]{:S(2)}) copy-start(bf16[32,1024]{1,0:T(8,128)(2,1)} %param.13) | copy-start | bytes 196612
  8.1 24.1 %all-to-all-start = ((s32[3,64,16]{2,0,1:T(4,128)}), s32[3,64,16]{2,0,1:T(4,128)S(1)}, u32[]{:S(2)}, u32[]{:S(2)}) async-start(s32[3,64,16]{2,0,1:T(4,128)} %copy.56), calls=%async_computation | async-start | bytes 262144 | tf_op jit(solution)/shard_map/all_to_all | solution.py:95
  32.2 15.8 %all-to-all-start.1 = ((bf16[8,64,16]{2,0,1:T(8,128)(2,1)}), bf16[8,64,16]{2,0,1:T(8,128)(2,1)S(1)}, u32[]{:S(2)}, u32[]{:S(2)}) async-start(bf16[8,64,16]{2,0,1:T(8,128)(2,1)} %copy.58), calls=%async_computation.1 | async-start | bytes 262144 | tf_op jit(solution)/shard_map/all_to_all | solution.py:92
  69.7 8.3 %collective-permute-start = (f32[8,1,128,128]{3,2,1,0:T(8,128)S(1)}, f32[8,1,128,128]{3,2,1,0:T(8,128)S(1)}, u32[]{:S(2)}, u32[]{:S(2)}) collective-permute-start(f32[8,1,128,128]{3,2,1,0:T(8,128)S(1)} %slice.92), channel_id=1, source_target_pairs={{0,4},{4,8},{8,12},{12,16},{16,20},{20,24},{24,28},{28,32},{32,36}... | collective-permute-start | bytes 1572872 | tf_op jit(solution)/shard_map/ppermute | solution.py:19
  82.8 21.9 %all-to-all-start.2 = ((f32[64,1,1024]{2,1,0:T(1,128)}), f32[64,1,1024]{2,1,0:T(1,128)S(1)}, u32[]{:S(2)}, u32[]{:S(2)}) async-start(f32[64,1,1024]{2,1,0:T(1,128)} %reshape.293), calls=%async_computation.2 | async-start | bytes 524288 | tf_op jit(solution)/shard_map/all_to_all | solution.py:139
  91.5 73.9 %all-gather.2.cloned.1.call-start = ((), (), s32[]{:S(2)}) async-start(), calls=%async_computation.5 | async-start | bytes 2621440 | tf_op jit(solution)/shard_map/all_gather | solution.py:176
  140.1 25.3 %copy-start.1 = (bf16[32,8]{0,1:T(8,128)(2,1)S(1)}, bf16[32,8]{0,1:T(8,128)(2,1)}, u32[]{:S(2)}) copy-start(bf16[32,8]{0,1:T(8,128)(2,1)} %param.18) | copy-start | bytes 1540
  141.4 18.4 %all-to-all-start.3 = ((f32[64,1,1024]{2,1,0:T(1,128)}), f32[64,1,1024]{2,1,0:T(1,128)S(1)}, u32[]{:S(2)}, u32[]{:S(2)}) async-start(f32[64,1,1024]{2,1,0:T(1,128)} %reshape.295), calls=%async_computation.3 | async-start | bytes 524288 | tf_op jit(solution)/shard_map/all_to_all | solution.py:157
  161.0 7.2 %copy-start.4 = (f32[8]{0:T(128)S(1)}, f32[8]{0:T(128)}, u32[]{:S(2)}) copy-start(f32[8]{0:T(128)} %param.19) | copy-start | bytes 100
  170.6 7.7 %collective-permute-start.1 = (bf16[8,1,128,128]{3,2,1,0:T(8,128)(2,1)S(1)}, bf16[8,1,128,128]{3,2,1,0:T(8,128)(2,1)S(1)}, u32[]{:S(2)}, u32[]{:S(2)}) collective-permute-start(bf16[8,1,128,128]{3,2,1,0:T(8,128)(2,1)S(1)} %slice.102), channel_id=1, source_target_pairs={{4,0},{8,4},{12,8},{16,12},{20,16},{24,20},{28,24},{32,28},{36,32}... | collective-permute-start | bytes 786440 | tf_op jit(solution)/shard_map/ppermute | solution.py:19
  178.4 11.5 %copy-start.2 = (bf16[8,4]{0,1:T(4,128)(2,1)S(1)}, bf16[8,4]{0,1:T(4,128)(2,1)}, u32[]{:S(2)}) copy-start(bf16[8,4]{0,1:T(4,128)(2,1)} %param.20) | copy-start | bytes 196
  178.5 45.4 %copy-start.3 = (f32[4]{0:T(128)S(1)}, f32[4]{0:T(128)}, u32[]{:S(2)}) copy-start(f32[4]{0:T(128)} %param.21) | copy-start | bytes 52
Sparse Core Ops, SparseCore 0:
  94.1 42.8 all-gather.1
where the time goes:
time: 232 us; the launch traced here: 231 us
  blocking collectives  55.2 us (24%)
  waiting for transfers between devices  54.8 us (24%)
  matrix products  42.2 us (18%)
  starting transfers between devices  35.9 us (15%)
  other arithmetic  18.2 us (8%)
  between operations  14 us (6%)
  local copies, waits for them, and re-layouts  10.9 us (5%)
    all_gather x1, blocking collectives, local(): piece = lax.all_gather(spectra, 'chan', axis=1, tiled=True)  21.8 us
    all_to_all x1, blocking collectives, local(): lax.all_to_all(heads.reshape(nout, slabs, capacity), 'slab', split_axis=1...  19 us
    psum x1, blocking collectives, local(): heads = lax.psum(partial_heads, 'chan')  14.4 us
    dot_general x2, matrix products, deposit(): jnp.einsum('ab,zb->az', spread, z_block, precision=highest)  14.3 us
    all_to_all x1, waiting for transfers between devices, local(): lax.all_to_all(inverted, 'slab', split_axis=1, concat_axis=2, tiled=True)  13.1 us
    all_to_all x1, starting transfers between devices, local(): lax.all_to_all(cell_coords.reshape(3, slabs, capacity), 'slab', split_axi...  13 us
    all_to_all x1, waiting for transfers between devices, local(): lax.all_to_all(partly, 'slab', split_axis=2, concat_axis=1, tiled=True)  12.1 us
    ppermute x2, waiting for transfers between devices, passed_along(): return lax.ppermute(value, axis, pairs)  11.4 us
  transfers between devices with their start and end apart: 7, of which 6 were waited for; matrix products, arithmetic and copies ran while one was open for 11% of the time, Pallas kernels for 0%

commit v1 on v0

v1 whole, which is shorter than its diff:
```python
import functools
import math

import jax
import jax.numpy as jnp
import numpy as np
from jax import lax
from jax.experimental import pallas as pl
from jax.experimental.pallas import tpu as pltpu
from jax.sharding import PartitionSpec as P

GRID = 128
MZ = 32
CAP = 16
SLABS = 64
CHANS = 4
POINTS = 1024
MODES = np.concatenate([np.arange(MZ), np.arange(GRID - MZ, GRID)])
MESH = pl.DeviceIdType.MESH
F32 = jnp.float32
BF16 = jnp.bfloat16


def wave(freqs, positions):
    angle = (freqs[:, None] * positions[None, :] % GRID) * (2.0 * math.pi / GRID)
    return np.cos(angle), np.sin(angle)


def tables():
    spots = np.arange(GRID)
    cos_y, sin_y = wave(MODES, spots)
    cos_z, sin_z = wave(np.arange(MZ), spots)
    forward_y = np.concatenate([cos_y, -sin_y], axis=0)
    forward_z = np.concatenate([cos_z, -sin_z], axis=0)
    planes = np.arange(SLABS)[:, None] * 2 + np.arange(4)[None, :]
    cos_x, sin_x = wave(MODES, planes.reshape(-1) % GRID)
    cos_x = cos_x.reshape(64, SLABS, 4)
    sin_x = sin_x.reshape(64, SLABS, 4)
    forward_x = np.zeros((2, 2, 64, SLABS, 2, 4, 2))
    inverse_x = np.zeros((SLABS, 2, 2, 2, 2, 2, 64))
    for half in range(2):
        for plane in range(3):
            c, s = cos_x[:, :, plane], sin_x[:, :, plane]
            forward_x[0, half, :, :, half, plane, 0] = c
            forward_x[0, half, :, :, half, plane, 1] = s
            forward_x[1, half, :, :, half, plane, 0] = -s
            forward_x[1, half, :, :, half, plane, 1] = c
            if plane < 2:
                inverse_x[:, half, plane, 0, half, 0] = c.T
                inverse_x[:, half, plane, 0, half, 1] = -s.T
                inverse_x[:, half, plane, 1, half, 0] = s.T
                inverse_x[:, half, plane, 1, half, 1] = c.T
    inverse_y = np.block([[cos_y.T, -sin_y.T], [sin_y.T, cos_y.T]])
    factor = np.where(np.arange(MZ) == 0, 1.0, 2.0)[:, None] / float(GRID) ** 3
    inverse_z = np.zeros((2, 4, MZ, 4, GRID))
    for group in range(4):
        inverse_z[0, group, :, group] = factor * cos_z
        inverse_z[1, group, :, group] = -factor * sin_z
    as_bf16 = lambda table, shape: np.asarray(table.reshape(shape), dtype=jnp.bfloat16)
    return (
        as_bf16(forward_y, (128, 128)),
        as_bf16(forward_z, (64, 128)),
        as_bf16(forward_x, (256, 1024)),
        as_bf16(inverse_x, (512, 256)),
        as_bf16(inverse_y, (256, 128)),
        as_bf16(inverse_z, (256, 512)),
    )


def dot(a, b):
    return jnp.dot(a, b, preferred_element_type=F32)


def dot_nt(a, b):
    return lax.dot_general(a, b, (((1,), (1,)), ((), ())), preferred_element_type=F32)


def hat(spots, position):
    return jnp.maximum(1.0 - jnp.abs(spots - position), 0.0)


def iota(shape, dim):
    return lax.broadcasted_iota(jnp.int32, shape, dim)


def exchange(src, dst, send_sem, recv_sem, me, chan):
    def send(k, carry):
        to = lax.rem(me + k, SLABS)
        pltpu.make_async_remote_copy(
            src_ref=src.at[to],
            dst_ref=dst.at[me],
            send_sem=send_sem,
            recv_sem=recv_sem,
            device_id=(to, chan),
            device_id_type=MESH,
        ).start()
        return carry

    lax.fori_loop(1, SLABS, send, 0)
    dst[pl.ds(me, 1)] = src[pl.ds(me, 1)]


def all_but_one(src, dst, send_sem, recv_sem, me, chan):
    return pltpu.make_async_remote_copy(
        src_ref=src.at[pl.ds(0, SLABS - 1)],
        dst_ref=dst.at[pl.ds(0, SLABS - 1)],
        send_sem=send_sem,
        recv_sem=recv_sem,
        device_id=(me, chan),
        device_id_type=MESH,
    )


def kernel(
    feats, coords, counts, lift, weight, skip, bias, head, head_bias,
    fwd_y, fwd_z, fwd_x, inv_x, inv_y, inv_z,
    out,
    a_send, a_recv, t_ref, own, embeds, packet, before,
    hat_y, xz, yh, lhs, rhs, stage, c_send, c_recv,
    raw, packed, d_recv, acc, e_send, e_recv, mid, skipped, spectral,
    hn, heads, back, h_send, h_recv, sums,
    w_sem, a_sem, c_sem, e_sem, h_sem, n_sem, m_send, m_recv, d_send, d_rsem, g_send, g_recv,
):
    me = lax.axis_index("slab")
    chan = lax.axis_index("chan")
    after = lax.rem(me + 1, SLABS)

    barrier = pltpu.get_barrier_semaphore()

    def greet(k, carry):
        to = lax.rem(me + k, SLABS)
        pl.semaphore_signal(barrier, inc=1, device_id=(to, chan), device_id_type=MESH)
        return carry

    lax.fori_loop(1, SLABS, greet, 0)
    for k in range(1, CHANS):
        pl.semaphore_signal(
            barrier, inc=1, device_id=(me, lax.rem(chan + k, CHANS)), device_id_type=MESH
        )
    load = pltpu.make_async_copy(weight, raw, w_sem)
    load.start()

    lane = iota((16, POINTS), 1)
    mask = jnp.where((lane & 15) == iota((16, POINTS), 0), 1.0, 0.0)
    pick = jnp.where((iota((SLABS, POINTS), 1) >> 4) == iota((SLABS, POINTS), 0), 1.0, 0.0).astype(BF16)
    embed = dot(lift[...], feats[...]).astype(BF16).astype(F32)
    spot = coords[...]
    cell = (spot >> 4).astype(F32)
    part = (spot & 15).astype(F32)
    rows = [embed[v : v + 1] for v in range(8)]
    rows += [cell[v : v + 1] for v in range(3)] + [part[v : v + 1] for v in range(3)]
    spread = [(row * mask).astype(BF16) for row in rows]
    spread += [jnp.zeros((32, POINTS), BF16)]
    sorted_ = dot_nt(pick, jnp.concatenate(spread, axis=0))
    wide = jnp.broadcast_to(counts[...].astype(F32), (SLABS, SLABS))
    here = jnp.sum(jnp.where(iota((SLABS, SLABS), 0) == iota((SLABS, SLABS), 1), wide, 0.0), axis=1, keepdims=True)
    live = (iota((SLABS, 128), 1) & 15).astype(F32) < here
    a_send[:, 0:1, :] = jnp.where(live, sorted_[:, :128], 0.0).reshape(SLABS, 1, 128)
    a_send[:, 1:2, :] = sorted_[:, 128:].reshape(SLABS, 1, 128)

    pl.semaphore_wait(barrier, SLABS - 1 + CHANS - 1)
    exchange(a_send, a_recv, a_sem.at[0], a_sem.at[1], me, chan)
    all_but_one(a_send, a_recv, a_sem.at[0], a_sem.at[1], me, chan).wait_recv()

    got = a_recv[...]
    t_ref[...] = jnp.concatenate(
        [got[:, 0:1, :].reshape(SLABS, 128), got[:, 1:2, :].reshape(SLABS, 128)], axis=0
    ).T
    low = iota((8, 128), 1) < 64
    for k in range(8):
        first = t_ref[pl.ds(k, 8, stride=16), :]
        second = t_ref[pl.ds(k + 8, 8, stride=16), :]
        values = jnp.where(low, first, pltpu.roll(second, 64, 1))
        places = jnp.where(low, pltpu.roll(first, 64, 1), second)
        lanes = pl.ds(k * 128, 128)
        own[0:8, lanes] = values
        own[8:11, lanes] = places[0:3] + (places[3:6] + 0.5) * 0.0625
    embeds[pl.ds(chan, 1)] = own[0:8, :].reshape(1, 8, POINTS)
    for k in range(1, CHANS):
        pltpu.make_async_remote_copy(
            src_ref=own.at[0:8],
            dst_ref=embeds.at[chan],
            send_sem=m_send.at[k],
            recv_sem=m_recv.at[k],
            device_id=(me, lax.rem(chan + k, CHANS)),
            device_id_type=MESH,
        ).start()

    down = iota((128, POINTS), 0).astype(F32)
    hat_own = hat(down, own[9:10, :]).astype(BF16)
    hat_y[:, 0:POINTS] = hat_own
    hat_z = hat(down, own[10:11, :]).astype(BF16)
    yh[0:128, :] = dot(fwd_y[...], hat_own)
    yh[128:192, :] = dot(fwd_z[...], hat_z)
    base = (me * 2).astype(F32)
    local = own[8:9, :] - base
    inside = jnp.where(me == SLABS - 1, 0.0, 1.0).astype(F32)
    for plane in range(3):
        along = hat(float(plane), local)
        if plane == 2:
            along = along * inside
        for part_ in range(2):
            lhs[plane * 64 : plane * 64 + 64, part_ * POINTS : (part_ + 1) * POINTS] = (
                yh[part_ * 64 : part_ * 64 + 64, :] * along
            ).astype(BF16)
    zr = yh[128:160, :]
    zi = yh[160:192, :]
    for c in range(8):
        row = own[c : c + 1, :]
        real = (zr * row).astype(BF16)
        imag = (zi * row).astype(BF16)
        rhs[c * 32 : c * 32 + 32, 0:POINTS] = real
        rhs[c * 32 : c * 32 + 32, POINTS : 2 * POINTS] = -imag
        rhs[256 + c * 32 : 256 + c * 32 + 32, 0:POINTS] = imag
        rhs[256 + c * 32 : 256 + c * 32 + 32, POINTS : 2 * POINTS] = real
    stage[...] = jnp.zeros_like(stage)
    for part_ in range(2):
        for half in range(2):
            block = part_ * 2 + half
            result = dot_nt(lhs[...], rhs[block * 128 : block * 128 + 128, :])
            for plane in range(3):
                stage[pl.ds(half * 8 + plane * 2 + part_, 64, stride=16), :] = result[
                    plane * 64 : plane * 64 + 64
                ]
    c_send[...] = stage[...].reshape(SLABS, 16, 128).astype(BF16)
    exchange(c_send, c_recv, c_sem.at[0], c_sem.at[1], me, chan)

    for k in range(1, CHANS):
        pltpu.make_async_remote_copy(
            src_ref=own.at[0:8],
            dst_ref=embeds.at[lax.rem(chan + CHANS - k, CHANS)],
            send_sem=m_send.at[k],
            recv_sem=m_recv.at[k],
            device_id=(me, chan),
            device_id_type=MESH,
        ).wait_recv()
    packet[0:8, :] = dot(skip[...], embeds[...].reshape(32, POINTS).astype(BF16))
    packet[8:16, :] = own[8:16, :]
    pass_on = pltpu.make_async_remote_copy(
        src_ref=packet,
        dst_ref=before,
        send_sem=n_sem.at[0],
        recv_sem=n_sem.at[1],
        device_id=(after, chan),
        device_id_type=MESH,
    )
    pass_on.start()
    for plane in range(2):
        xz[plane * 128 : plane * 128 + 128, 0:POINTS] = (
            hat(float(plane), local) * hat(down, own[10:11, :])
        ).astype(BF16)
    load.wait()

    def pack(step, carry):
        kind = step // 16
        rest = step % 16
        source = (rest // 4) * 8 + rest % 4
        one = raw[kind, source]
        two = raw[kind, source + 4]
        packed[kind, rest] = jnp.concatenate([one, two], axis=-1)
        return carry

    lax.fori_loop(0, 32, pack, 0)
    all_but_one(c_send, c_recv, c_sem.at[0], c_sem.at[1], me, chan).wait_recv()

    modes = dot(fwd_x[...], c_recv[...].reshape(1024, 128))
    turned = jnp.concatenate([modes[0:128].T, modes[128:256].T], axis=0).astype(BF16)
    d_recv[pl.ds(chan, 1)] = turned.reshape(1, 256, 128)

    def gather(k, owner, to):
        return pltpu.make_async_remote_copy(
            src_ref=d_recv.at[owner],
            dst_ref=d_recv.at[owner],
            send_sem=d_send.at[k],
            recv_sem=d_rsem.at[k],
            device_id=(me, to),
            device_id_type=MESH,
        )

    for k in range(1, CHANS):
        gather(k, chan, lax.rem(chan + k, CHANS)).start()

    pass_on.wait_recv()
    hat_y[:, POINTS : 2 * POINTS] = hat(down, before[9:10, :]).astype(BF16)
    prior = before[8:9, :] - base
    for plane in range(2):
        xz[plane * 128 : plane * 128 + 128, POINTS : 2 * POINTS] = (
            hat(float(plane), prior) * hat(down, before[10:11, :])
        ).astype(BF16)

    for k in range(CHANS):
        owner = lax.rem(chan + CHANS - k, CHANS)
        if k:
            gather(k, owner, chan).wait_recv()
        def mix(o, carry, k=k, owner=owner):
            if k:
                real, imag = acc[0, o], acc[1, o]
            else:
                real = imag = jnp.zeros((MZ, 128), F32)
            for group in range(4):
                at = owner * 4 + group
                wr, wi = packed[0, at, o], packed[1, at, o]
                vr = d_recv[owner, group * 32 : group * 32 + 32, :].astype(F32)
                vi = d_recv[owner, 128 + group * 32 : 128 + group * 32 + 32, :].astype(F32)
                real = real + (wr * vr - wi * vi)
                imag = imag + (wr * vi + wi * vr)
            acc[0, o] = real
            acc[1, o] = imag
            return carry

        lax.fori_loop(0, 8, mix, 0)
    low = iota((MZ, 128), 1) < 64
    mixed = []
    for o in range(8):
        real, imag = acc[0, o], acc[1, o]
        real = real + pltpu.roll(real, 64, 1)
        imag = imag + pltpu.roll(imag, 64, 1)
        mixed.append(jnp.where(low, real, imag).astype(BF16))
    mixed = jnp.concatenate(
        [jnp.concatenate(mixed[0:4], axis=0), jnp.concatenate(mixed[4:8], axis=0)], axis=1
    )
    e_send[...] = dot_nt(inv_x[...], mixed).reshape(SLABS, 8, 128)
    exchange(e_send, e_recv, e_sem.at[0], e_sem.at[1], me, chan)

    def deposit(o, carry):
        spread = jnp.concatenate(
            [
                (packet[pl.ds(o, 1), :] * hat_y[:, 0:POINTS].astype(F32)).astype(BF16),
                (before[pl.ds(o, 1), :] * hat_y[:, POINTS : 2 * POINTS].astype(F32)).astype(BF16),
            ],
            axis=1,
        )
        skipped[o] = dot_nt(spread, xz[...]) + bias[o]
        return carry

    lax.fori_loop(0, 8, deposit, 0)
    all_but_one(e_send, e_recv, e_sem.at[0], e_sem.at[1], me, chan).wait_recv()

    for row in range(8):
        block, part_ = row // 2, row % 2
        mid[part_ * 64 : part_ * 64 + 64, block * 128 : block * 128 + 128] = (
            e_recv[:, row : row + 1, :].reshape(SLABS, 128).astype(BF16)
        )
    lines = dot(inv_y[...], mid[...]).astype(BF16)
    for half in range(2):
        for plane in range(2):
            block = half * 2 + plane
            both = jnp.concatenate(
                [
                    lines[0:128, block * 128 : block * 128 + 128],
                    lines[128:256, block * 128 : block * 128 + 128],
                ],
                axis=1,
            )
            result = dot(both, inv_z[...])
            for group in range(4):
                spectral[half * 4 + group, :, plane * 128 : plane * 128 + 128] = result[
                    :, group * 128 : group * 128 + 128
                ]

    heading = head[...].astype(F32)
    shape = (32, 256)
    scale = math.sqrt(2.0 / math.pi)

    def activate(step, carry):
        at = pl.ds(step * 32, 32)
        fields = [jnp.zeros(shape, F32) for _ in range(4)]
        for o in range(8):
            x = spectral[o, at, :] + skipped[o, at, :]
            h = 0.5 * x * (1.0 + jnp.tanh(scale * (x + 0.044715 * (x * x * x))))
            for n in range(4):
                fields[n] = fields[n] + jnp.broadcast_to(heading[n : n + 1, o : o + 1], shape) * h
        for n in range(4):
            hn[n, at, :] = fields[n].astype(BF16)
        return carry

    lax.fori_loop(0, 4, activate, 0)

    fields = hn[...].reshape(512, 256)
    for block in range(8):
        lanes = pl.ds(block * 256, 256)
        along_z = dot(fields, xz[:, lanes])
        weights = hat_y[:, lanes].astype(F32)
        for n in range(4):
            sampled = jnp.sum(along_z[n * 128 : n * 128 + 128] * weights, axis=0, keepdims=True)
            which = block // 4
            heads[which * 4 + n : which * 4 + n + 1, pl.ds((block % 4) * 256, 256)] = sampled
    for k in range(8):
        piece = heads[:, k * 128 : k * 128 + 128]
        back[pl.ds(k, 8, stride=16), :] = piece
        back[pl.ds(k + 8, 8, stride=16), :] = pltpu.roll(piece, 64, 1)
    h_send[...] = back[...].T[0:SLABS].reshape(SLABS, 1, 128)
    exchange(h_send, h_recv, h_sem.at[0], h_sem.at[1], me, chan)
    all_but_one(h_send, h_recv, h_sem.at[0], h_sem.at[1], me, chan).wait_recv()

    home = h_recv[...].reshape(SLABS, 128)
    home = home + pltpu.roll(pltpu.roll(home, SLABS - 1, 0), 64, 1)
    sums[pl.ds(chan, 1)] = home.reshape(1, SLABS, 128)

    def total(k, owner, to):
        return pltpu.make_async_remote_copy(
            src_ref=sums.at[owner],
            dst_ref=sums.at[owner],
            send_sem=g_send.at[k],
            recv_sem=g_recv.at[k],
            device_id=(me, to),
            device_id_type=MESH,
        )

    for k in range(1, CHANS):
        total(k, chan, lax.rem(chan + k, CHANS)).start()
    pick2 = jnp.where((iota((SLABS, POINTS), 1) >> 4) == iota((SLABS, POINTS), 0), 1.0, 0.0).astype(BF16)
    cover = dot(jnp.broadcast_to(counts[...].astype(F32), (8, SLABS)).astype(BF16), pick2)
    alive = (iota((4, POINTS), 1) & 15).astype(F32) < cover[0:4]
    for k in range(1, CHANS):
        total(k, lax.rem(chan + CHANS - k, CHANS), chan).wait_recv()
    home = sums[0] + sums[1] + sums[2] + sums[3]
    turned = jnp.concatenate([home, jnp.zeros_like(home)], axis=0).T[0:SLABS, 0:SLABS]
    top = turned.astype(BF16)
    rest = turned - top.astype(F32)
    middle = rest.astype(BF16)
    bottom = (rest - middle.astype(F32)).astype(BF16)
    laid = dot(top, pick2) + dot(middle, pick2) + dot(bottom, pick2)
    for n in range(4):
        line = jnp.sum(laid[n * 16 : n * 16 + 16] * mask, axis=0, keepdims=True)
        out[n : n + 1, :] = jnp.where(alive[n : n + 1], line + head_bias[n], 0.0)

    for pair, src, dst in ((a_sem, a_send, a_recv), (c_sem, c_send, c_recv), (e_sem, e_send, e_recv), (h_sem, h_send, h_recv)):
        all_but_one(src, dst, pair.at[0], pair.at[1], me, chan).wait_send()
    pass_on.wait_send()
    for k in range(1, CHANS):
        pltpu.make_async_remote_copy(
            src_ref=own.at[0:8],
            dst_ref=embeds.at[chan],
            send_sem=m_send.at[k],
            recv_sem=m_recv.at[k],
            device_id=(me, chan),
            device_id_type=MESH,
        ).wait_send()
        gather(k, chan, chan).wait_send()
        total(k, chan, chan).wait_send()


def local(
    point_feats, cell_coords, send_counts, lift_weight, spec_weight,
    skip_weight, spec_bias, out_weight, out_bias,
):
    weight = jnp.swapaxes(spec_weight, 4, 5).reshape(2, 32, 8, MZ, 64)
    vmem = pl.BlockSpec(memory_space=pltpu.VMEM)
    smem = pl.BlockSpec(memory_space=pltpu.SMEM)
    hbm = pl.BlockSpec(memory_space=pl.ANY)
    dma = pltpu.SemaphoreType.DMA
    scratch = [
        pltpu.VMEM((SLABS, 2, 128), F32),
        pltpu.VMEM((SLABS, 2, 128), F32),
        pltpu.VMEM((128, 128), F32),
        pltpu.VMEM((16, POINTS), F32),
        pltpu.VMEM((CHANS, 8, POINTS), F32),
        pltpu.VMEM((16, POINTS), F32),
        pltpu.VMEM((16, POINTS), F32),
        pltpu.VMEM((128, 2 * POINTS), BF16),
        pltpu.VMEM((256, 2 * POINTS), BF16),
        pltpu.VMEM((192, POINTS), F32),
        pltpu.VMEM((192, 2 * POINTS), BF16),
        pltpu.VMEM((512, 2 * POINTS), BF16),
        pltpu.VMEM((1024, 128), F32),
        pltpu.VMEM((SLABS, 16, 128), BF16),
        pltpu.VMEM((SLABS, 16, 128), BF16),
        pltpu.VMEM((2, 32, 8, MZ, 64), F32),
        pltpu.VMEM((2, 16, 8, MZ, 128), F32),
        pltpu.VMEM((CHANS, 256, 128), BF16),
        pltpu.VMEM((2, 8, MZ, 128), F32),
        pltpu.VMEM((SLABS, 8, 128), F32),
        pltpu.VMEM((SLABS, 8, 128), F32),
        pltpu.VMEM((128, 512), BF16),
        pltpu.VMEM((8, 128, 256), F32),
        pltpu.VMEM((8, 128, 256), F32),
        pltpu.VMEM((4, 128, 256), BF16),
        pltpu.VMEM((8, POINTS), F32),
        pltpu.VMEM((128, 128), F32),
        pltpu.VMEM((SLABS, 1, 128), F32),
        pltpu.VMEM((SLABS, 1, 128), F32),
        pltpu.VMEM((CHANS, SLABS, 128), F32),
        dma,
        dma((2,)),
        dma((2,)),
        dma((2,)),
        dma((2,)),
        dma((2,)),
        dma((CHANS,)),
        dma((CHANS,)),
        dma((CHANS,)),
        dma((CHANS,)),
        dma((CHANS,)),
        dma((CHANS,)),
    ]
    return pl.pallas_call(
        kernel,
        out_shape=jax.ShapeDtypeStruct((4, POINTS), F32),
        in_specs=[vmem, vmem, vmem, vmem, hbm, vmem, smem, vmem, smem] + [vmem] * 6,
        out_specs=vmem,
        scratch_shapes=scratch,
        compiler_params=pltpu.CompilerParams(
            collective_id=0, has_side_effects=True, vmem_limit_bytes=48 * 1024 * 1024
        ),
    )(
        point_feats, cell_coords, send_counts, lift_weight.T, weight,
        skip_weight.T, spec_bias, out_weight.T, out_bias, *(jnp.asarray(t) for t in tables()),
    )


def solution(mesh):
    in_specs = (
        P(None, "slab"),
        P(None, "slab"),
        P("slab", None),
        P(None, "chan"),
        P(None, None, "chan", "slab", None, None),
        P(None, "chan"),
        P("chan"),
        P("chan", None),
        P(),
    )
    out_specs = P(None, "slab")
    return jax.shard_map(local, mesh=mesh, in_specs=in_specs, out_specs=out_specs, check_vma=False)
```

time: 232 us -> 70.3 us (0.30)
  Pallas kernels: 0 us -> 58.3 us
  blocking collectives: 55.2 us -> 0 us
  waiting for transfers between devices: 54.8 us -> 0 us
  matrix products: 42.2 us -> 0 us
  starting transfers between devices: 35.9 us -> 0 us
  other arithmetic: 18.2 us -> 0 us
  between operations: 14 us -> 0.02 us
    pallas_call x0 -> x1, Pallas kernels: none -> 58.3 us  [local(): pl.pallas_call(kernel, out_shape=jax.ShapeDtypeStruct((4, POINTS), F32),...]
    all_to_all x4 -> x0, waiting for transfers between devices: 43.4 us -> none  [the longest x1 13.1 us: local(): lax.all_to_all(inverted, 'slab', split_axis=1, concat_axis=2, tiled=True)]
    dot_general x26 -> x0, matrix products: 42.2 us -> none  [the longest x2 14.3 us: deposit(): jnp.einsum('ab,zb->az', spread, z_block, precision=highest)]
    all_to_all x4 -> x0, starting transfers between devices: 31.4 us -> none  [the longest x1 13 us: local(): lax.all_to_all(cell_coords.reshape(3, slabs, capacity), 'slab', split_axi...]
    all_gather x1 -> x0, blocking collectives: 21.8 us -> none  [local(): piece = lax.all_gather(spectra, 'chan', axis=1, tiled=True)]
    all_to_all x1 -> x0, blocking collectives: 19 us -> none  [local(): lax.all_to_all(heads.reshape(nout, slabs, capacity), 'slab', split_axis=1...]
    psum x1 -> x0, blocking collectives: 14.4 us -> none  [local(): heads = lax.psum(partial_heads, 'chan')]
    ppermute x2 -> x0, waiting for transfers between devices: 11.4 us -> none  [passed_along(): return lax.ppermute(value, axis, pairs)]
  transfers between devices with their start and end apart: 7 -> 0, of which waited for: 6 -> 0; matrix products, arithmetic and copies ran while one was open for 11% -> 0% of each run, Pallas kernels for 0% -> 0%
where the time goes in v1:
time: 70.3 us; the launch traced here: 69.8 us
  Pallas kernels  58.3 us (83%)
  local copies, waits for them, and re-layouts  11.4 us (16%)
    pallas_call x1, Pallas kernels, local(): pl.pallas_call(kernel, out_shape=jax.ShapeDtypeStruct((4, POINTS), F32),...  58.3 us
    unnamed x29, local copies, waits for them, and re-layouts  11.4 us

profile of v1, /device:TPU:1, one launch (start us, length us, event | category | flops | bytes accessed | tf_op | source)
XLA Modules:
  0.0 69.8 jit_solution(1554217636213547422)
XLA Ops:
  0.0 0.0 copy-start
  0.0 1.0 %copy-done = bf16[256,1024]{1,0:T(8,128)(2,1)S(1)} copy-done((bf16[256,1024]{1,0:T(8,128)(2,1)S(1)}, bf16[256,1024]{1,0:T(8,128)(2,1)}, u32[]{:S(2)}) %copy-start) | copy-done | bytes 524312
  1.0 0.0 copy-start.1
  1.0 0.9 %copy-done.1 = bf16[256,512]{1,0:T(8,128)(2,1)S(1)} copy-done((bf16[256,512]{1,0:T(8,128)(2,1)S(1)}, bf16[256,512]{1,0:T(8,128)(2,1)}, u32[]{:S(2)}) %copy-start.1) | copy-done | bytes 262168
  2.0 0.0 copy-start.2
  2.0 0.9 %copy-done.2 = bf16[512,256]{1,0:T(8,128)(2,1)S(1)} copy-done((bf16[512,256]{1,0:T(8,128)(2,1)S(1)}, bf16[512,256]{1,0:T(8,128)(2,1)}, u32[]{:S(2)}) %copy-start.2) | copy-done | bytes 262168
  2.9 0.0 copy-start.3
  2.9 0.8 %copy-done.3 = bf16[32,1024]{1,0:T(8,128)(2,1)S(1)} copy-done((bf16[32,1024]{1,0:T(8,128)(2,1)S(1)}, bf16[32,1024]{1,0:T(8,128)(2,1)}, u32[]{:S(2)}) %copy-start.3) | copy-done | bytes 65560
  3.8 0.0 copy-start.4
  3.8 0.8 %copy-done.4 = bf16[256,128]{1,0:T(8,128)(2,1)S(1)} copy-done((bf16[256,128]{1,0:T(8,128)(2,1)S(1)}, bf16[256,128]{1,0:T(8,128)(2,1)}, u32[]{:S(2)}) %copy-start.4) | copy-done | bytes 65560
  4.6 0.0 copy-start.5
  4.6 0.8 %copy-done.5 = bf16[128,128]{1,0:T(8,128)(2,1)S(1)} copy-done((bf16[128,128]{1,0:T(8,128)(2,1)S(1)}, bf16[128,128]{1,0:T(8,128)(2,1)}, u32[]{:S(2)}) %copy-start.5) | copy-done | bytes 32792
  5.4 0.0 copy-start.6
  5.4 0.7 %copy-done.6 = s32[3,1024]{1,0:T(4,128)S(1)} copy-done((s32[3,1024]{1,0:T(4,128)S(1)}, s32[3,1024]{1,0:T(4,128)}, u32[]{:S(2)}) %copy-start.6) | copy-done | bytes 12312
  6.1 0.0 copy-start.7
  6.1 0.7 %copy-done.7 = bf16[64,128]{1,0:T(8,128)(2,1)S(1)} copy-done((bf16[64,128]{1,0:T(8,128)(2,1)S(1)}, bf16[64,128]{1,0:T(8,128)(2,1)}, u32[]{:S(2)}) %copy-start.7) | copy-done | bytes 16408
  6.8 0.0 copy-start.8
  6.8 0.7 copy-done.8
  7.5 0.0 copy-start.9
  7.5 0.7 copy-done.9
  8.2 0.0 copy-start.10
  8.2 0.7 copy-done.10
  8.9 0.0 copy-start.11
  8.9 0.7 copy-done.11
  9.5 0.0 copy-start.12
  9.5 0.7 copy-done.12
  10.2 0.0 copy-start.13
  10.2 0.7 copy-done.13
  10.8 58.3 %shard_map.145 = f32[4,1024]{1,0:T(4,128)S(1)} custom-call(bf16[32,1024]{1,0:T(8,128)(2,1)S(1)} %copy-done.3, s32[3,1024]{1,0:T(4,128)S(1)} %copy-done.6, s32[1,64]{1,0:T(1,128)S(1)} %copy-done.11, bf16[8,32]{1,0:T(8,128)(2,1)S(1)} %bitcast.8, f32[2,32,8,32,64]{4,3,2,1,0:T(8,128)} %bitcast.11, bf16[8,32]{1,0:T(8,128)(2,1)S(1)} %bitcast.9, f32[8]{0:T(128)S(1)} %copy-done.12, ...), custom_call_target="tpu_custom_call" | custom-call | tf_op jit(solution)/shard_map/pallas_call | solution.py:497
  69.2 0.6 copy.18
Async XLA Ops:
  0.0 1.0 %copy-start = (bf16[256,1024]{1,0:T(8,128)(2,1)S(1)}, bf16[256,1024]{1,0:T(8,128)(2,1)}, u32[]{:S(2)}) copy-start(bf16[256,1024]{1,0:T(8,128)(2,1)} %constant.14.clone.fwd_x) | copy-start | bytes 1572868
  1.0 0.9 %copy-start.1 = (bf16[256,512]{1,0:T(8,128)(2,1)S(1)}, bf16[256,512]{1,0:T(8,128)(2,1)}, u32[]{:S(2)}) copy-start(bf16[256,512]{1,0:T(8,128)(2,1)} %constant.17.clone.inv_z) | copy-start | bytes 786436
  2.0 0.9 %copy-start.2 = (bf16[512,256]{1,0:T(8,128)(2,1)S(1)}, bf16[512,256]{1,0:T(8,128)(2,1)}, u32[]{:S(2)}) copy-start(bf16[512,256]{1,0:T(8,128)(2,1)} %constant.15.clone.inv_x) | copy-start | bytes 786436
  2.9 0.8 %copy-start.3 = (bf16[32,1024]{1,0:T(8,128)(2,1)S(1)}, bf16[32,1024]{1,0:T(8,128)(2,1)}, u32[]{:S(2)}) copy-start(bf16[32,1024]{1,0:T(8,128)(2,1)} %feats.1) | copy-start | bytes 196612
  3.8 0.8 %copy-start.4 = (bf16[256,128]{1,0:T(8,128)(2,1)S(1)}, bf16[256,128]{1,0:T(8,128)(2,1)}, u32[]{:S(2)}) copy-start(bf16[256,128]{1,0:T(8,128)(2,1)} %constant.16.clone.inv_y) | copy-start | bytes 196612
  4.6 0.8 %copy-start.5 = (bf16[128,128]{1,0:T(8,128)(2,1)S(1)}, bf16[128,128]{1,0:T(8,128)(2,1)}, u32[]{:S(2)}) copy-start(bf16[128,128]{1,0:T(8,128)(2,1)} %constant.12.clone.fwd_y) | copy-start | bytes 98308
  5.4 0.7 %copy-start.6 = (s32[3,1024]{1,0:T(4,128)S(1)}, s32[3,1024]{1,0:T(4,128)}, u32[]{:S(2)}) copy-start(s32[3,1024]{1,0:T(4,128)} %coords.1) | copy-start | bytes 36868
  6.1 0.7 %copy-start.7 = (bf16[64,128]{1,0:T(8,128)(2,1)S(1)}, bf16[64,128]{1,0:T(8,128)(2,1)}, u32[]{:S(2)}) copy-start(bf16[64,128]{1,0:T(8,128)(2,1)} %constant.13.clone.fwd_z) | copy-start | bytes 49156
  6.8 0.7 copy-start.8
  7.5 0.7 copy-start.9
  8.2 0.7 copy-start.10
  8.9 0.7 copy-start.11
  9.5 0.7 copy-start.12
  10.2 0.7 copy-start.13

commit v2 on v1

v2 whole, which is shorter than its diff:
```python
import functools
import math

import jax
import jax.numpy as jnp
import numpy as np
from jax import lax
from jax.experimental import pallas as pl
from jax.experimental.pallas import tpu as pltpu
from jax.sharding import PartitionSpec as P

GRID = 128
MZ = 32
CAP = 16
SLABS = 64
CHANS = 4
POINTS = 1024
MODES = np.concatenate([np.arange(MZ), np.arange(GRID - MZ, GRID)])
MESH = pl.DeviceIdType.MESH
F32 = jnp.float32
BF16 = jnp.bfloat16


def wave(freqs, positions):
    angle = (freqs[:, None] * positions[None, :] % GRID) * (2.0 * math.pi / GRID)
    return np.cos(angle), np.sin(angle)


def tables():
    spots = np.arange(GRID)
    cos_y, sin_y = wave(MODES, spots)
    cos_z, sin_z = wave(np.arange(MZ), spots)
    forward_y = np.concatenate([cos_y, -sin_y], axis=0)
    forward_z = np.concatenate([cos_z, -sin_z], axis=0)
    planes = np.arange(SLABS)[:, None] * 2 + np.arange(2)[None, :]
    cos_x, sin_x = wave(MODES, planes.reshape(-1) % GRID)
    cos_x = cos_x.reshape(64, SLABS, 2)
    sin_x = sin_x.reshape(64, SLABS, 2)
    forward_x = np.zeros((2, 2, 64, SLABS, 2, 2, 2))
    inverse_x = np.zeros((SLABS, 2, 2, 2, 2, 2, 64))
    for half in range(2):
        for plane in range(2):
            c, s = cos_x[:, :, plane], sin_x[:, :, plane]
            forward_x[0, half, :, :, half, plane, 0] = c
            forward_x[0, half, :, :, half, plane, 1] = s
            forward_x[1, half, :, :, half, plane, 0] = -s
            forward_x[1, half, :, :, half, plane, 1] = c
            inverse_x[:, half, plane, 0, half, 0] = c.T
            inverse_x[:, half, plane, 0, half, 1] = -s.T
            inverse_x[:, half, plane, 1, half, 0] = s.T
            inverse_x[:, half, plane, 1, half, 1] = c.T
    inverse_y = np.zeros((4, 2, GRID, 64, 4, 2))
    for block in range(4):
        inverse_y[block, 0, :, :, block, 0] = cos_y.T
        inverse_y[block, 0, :, :, block, 1] = -sin_y.T
        inverse_y[block, 1, :, :, block, 0] = sin_y.T
        inverse_y[block, 1, :, :, block, 1] = cos_y.T
    factor = np.where(np.arange(MZ) == 0, 1.0, 2.0)[:, None] / float(GRID) ** 3
    inverse_z = np.zeros((2, 4, MZ, 4, GRID))
    for group in range(4):
        inverse_z[0, group, :, group] = factor * cos_z
        inverse_z[1, group, :, group] = -factor * sin_z
    as_bf16 = lambda table, shape: np.asarray(table.reshape(shape), dtype=jnp.bfloat16)
    return (
        as_bf16(np.concatenate([forward_y, forward_z], axis=0), (192, 128)),
        as_bf16(forward_x, (256, 512)),
        as_bf16(inverse_x, (512, 256)),
        as_bf16(inverse_y, (1024, 512)),
        as_bf16(inverse_z, (256, 512)),
    )


def dot(a, b):
    return jnp.dot(a, b, preferred_element_type=F32)


def dot_nt(a, b):
    return lax.dot_general(a, b, (((1,), (1,)), ((), ())), preferred_element_type=F32)


def hat(spots, position):
    return jnp.maximum(1.0 - jnp.abs(spots - position), 0.0)


def iota(shape, dim):
    return lax.broadcasted_iota(jnp.int32, shape, dim)


def exchange(src, dst, send_sem, recv_sem, me, chan):
    def send(k, carry):
        to = lax.rem(me + k, SLABS)
        pltpu.make_async_remote_copy(
            src_ref=src.at[to],
            dst_ref=dst.at[me],
            send_sem=send_sem,
            recv_sem=recv_sem,
            device_id=(to, chan),
            device_id_type=MESH,
        ).start()
        return carry

    lax.fori_loop(1, SLABS, send, 0)
    dst[pl.ds(me, 1)] = src[pl.ds(me, 1)]


def all_but_one(src, dst, send_sem, recv_sem, me, chan):
    return pltpu.make_async_remote_copy(
        src_ref=src.at[pl.ds(0, SLABS - 1)],
        dst_ref=dst.at[pl.ds(0, SLABS - 1)],
        send_sem=send_sem,
        recv_sem=recv_sem,
        device_id=(me, chan),
        device_id_type=MESH,
    )


def kernel(
    feats_in, coords_in, counts_in, lift_in, weight, skip_in, bias_in, head_in, head_bias_in,
    fwd_yz_in, fwd_x_in, inv_x_in, inv_y_in, inv_z_in,
    out,
    feats, coords, counts, lift, skip, bias, head, head_bias,
    fwd_yz, fwd_x, inv_x, inv_y, inv_z,
    a_send, a_recv, t_ref, own, prior, embeds, packet, before, along,
    hat_y, hat_z, yh, lhs, rhs, stage, c_send, c_recv,
    raw, packed, d_recv, acc, e_send, e_recv, skipped, spectral,
    hn, heads, back, h_send, h_recv, sums,
    load_sem, a_sem, c_sem, e_sem, h_sem, n_sem, s_sem, m_send, m_recv, d_send, d_rsem, g_send, g_recv,
):
    me = lax.axis_index("slab")
    chan = lax.axis_index("chan")
    after = lax.rem(me + 1, SLABS)

    loads = {}
    for k, (name, src, dst) in enumerate((
        ("feats", feats_in, feats), ("coords", coords_in, coords), ("counts", counts_in, counts),
        ("lift", lift_in, lift), ("fwd_yz", fwd_yz_in, fwd_yz), ("skip", skip_in, skip),
        ("weight", weight, raw), ("fwd_x", fwd_x_in, fwd_x), ("inv_x", inv_x_in, inv_x),
        ("inv_y", inv_y_in, inv_y), ("inv_z", inv_z_in, inv_z), ("bias", bias_in, bias),
        ("head", head_in, head), ("head_bias", head_bias_in, head_bias),
    )):
        loads[name] = pltpu.make_async_copy(src, dst, load_sem.at[k])

    barrier = pltpu.get_barrier_semaphore()

    def greet(k, carry):
        to = lax.rem(me + k, SLABS)
        pl.semaphore_signal(barrier, inc=1, device_id=(to, chan), device_id_type=MESH)
        return carry

    lax.fori_loop(1, SLABS, greet, 0)
    for k in range(1, CHANS):
        pl.semaphore_signal(
            barrier, inc=1, device_id=(me, lax.rem(chan + k, CHANS)), device_id_type=MESH
        )
    for load in loads.values():
        load.start()
    pending = []
    for name in ("feats", "coords", "counts", "lift"):
        loads[name].wait()

    lane = iota((16, POINTS), 1)
    mask = jnp.where((lane & 15) == iota((16, POINTS), 0), 1.0, 0.0)
    pick = jnp.where((iota((SLABS, POINTS), 1) >> 4) == iota((SLABS, POINTS), 0), 1.0, 0.0).astype(BF16)
    embed = dot(lift[...], feats[...]).astype(BF16).astype(F32)
    spot = coords[...]
    cell = (spot >> 4).astype(F32)
    part = (spot & 15).astype(F32)
    rows = [embed[v : v + 1] for v in range(8)]
    rows += [cell[v : v + 1] for v in range(3)] + [part[v : v + 1] for v in range(3)]
    spread = [(row * mask).astype(BF16) for row in rows]
    spread += [jnp.zeros((32, POINTS), BF16)]
    sorted_ = dot_nt(pick, jnp.concatenate(spread, axis=0))
    wide = jnp.broadcast_to(counts[...].astype(F32), (SLABS, SLABS))
    here = jnp.sum(jnp.where(iota((SLABS, SLABS), 0) == iota((SLABS, SLABS), 1), wide, 0.0), axis=1, keepdims=True)
    live = (iota((SLABS, 128), 1) & 15).astype(F32) < here
    a_send[:, 0:1, :] = jnp.where(live, sorted_[:, :128], 0.0).reshape(SLABS, 1, 128)
    a_send[:, 1:2, :] = sorted_[:, 128:].reshape(SLABS, 1, 128)

    pl.semaphore_wait(barrier, SLABS - 1 + CHANS - 1)
    exchange(a_send, a_recv, a_sem.at[0], a_sem.at[1], me, chan)
    a_all = all_but_one(a_send, a_recv, a_sem.at[0], a_sem.at[1], me, chan)
    pending.append(a_all)
    a_all.wait_recv()

    got = a_recv[...]
    t_ref[...] = jnp.concatenate(
        [got[:, 0:1, :].reshape(SLABS, 128), got[:, 1:2, :].reshape(SLABS, 128)], axis=0
    ).T
    low = iota((8, 128), 1) < 64
    for k in range(8):
        first = t_ref[pl.ds(k, 8, stride=16), :]
        second = t_ref[pl.ds(k + 8, 8, stride=16), :]
        values = jnp.where(low, first, pltpu.roll(second, 64, 1))
        places = jnp.where(low, pltpu.roll(first, 64, 1), second)
        lanes = pl.ds(k * 128, 128)
        own[0:8, lanes] = values
        own[8:11, lanes] = places[0:3] + (places[3:6] + 0.5) * 0.0625
        own[11:16, lanes] = places[3:8]
    pass_on = pltpu.make_async_remote_copy(
        src_ref=own,
        dst_ref=prior,
        send_sem=n_sem.at[0],
        recv_sem=n_sem.at[1],
        device_id=(after, chan),
        device_id_type=MESH,
    )
    pass_on.start()
    pending.append(pass_on)
    embeds[pl.ds(chan, 1)] = own[0:8, :].reshape(1, 8, POINTS)

    def share(k, owner, to):
        return pltpu.make_async_remote_copy(
            src_ref=own.at[0:8],
            dst_ref=embeds.at[owner],
            send_sem=m_send.at[k],
            recv_sem=m_recv.at[k],
            device_id=(me, to),
            device_id_type=MESH,
        )

    for k in range(1, CHANS):
        share(k, chan, lax.rem(chan + k, CHANS)).start()
        pending.append(share(k, chan, chan))

    loads["fwd_yz"].wait()
    base = (me * 2).astype(F32)
    down = iota((128, POINTS), 0).astype(F32)

    def transform(points, which):
        lanes = slice(which * POINTS, (which + 1) * POINTS)
        hat_y[:, lanes] = hat(down, points[9:10, :]).astype(BF16)
        hat_z[:, lanes] = hat(down, points[10:11, :]).astype(BF16)
        yh[0:128, :] = dot(fwd_yz[0:128, :], hat_y[:, lanes])
        yh[128:192, :] = dot(fwd_yz[128:192, :], hat_z[:, lanes])
        local = points[8:9, :] - base
        planes = 2 - which
        for plane in range(planes):
            near = hat(float(plane), local)
            along[plane : plane + 1, lanes] = near
            for part_ in range(2):
                lhs[plane * 64 : plane * 64 + 64, part_ * POINTS : (part_ + 1) * POINTS] = (
                    yh[part_ * 64 : part_ * 64 + 64, :] * near
                ).astype(BF16)
        zr = yh[128:160, :]
        zi = yh[160:192, :]
        for c in range(8):
            row = points[c : c + 1, :]
            real = (zr * row).astype(BF16)
            imag = (zi * row).astype(BF16)
            rhs[c * 32 : c * 32 + 32, 0:POINTS] = real
            rhs[c * 32 : c * 32 + 32, POINTS : 2 * POINTS] = -imag
            rhs[256 + c * 32 : 256 + c * 32 + 32, 0:POINTS] = imag
            rhs[256 + c * 32 : 256 + c * 32 + 32, POINTS : 2 * POINTS] = real
        for part_ in range(2):
            for half in range(2):
                block = part_ * 2 + half
                result = dot_nt(lhs[0 : planes * 64], rhs[block * 128 : block * 128 + 128, :])
                for plane in range(planes):
                    rows = pl.ds(half * 4 + plane * 2 + part_, 64, stride=8)
                    piece = result[plane * 64 : plane * 64 + 64]
                    stage[rows, :] = stage[rows, :] + piece if which else piece

    transform(own, 0)
    pass_on.wait_recv()
    transform(prior, 1)
    c_send[...] = stage[...].reshape(SLABS, 8, 128).astype(BF16)
    exchange(c_send, c_recv, c_sem.at[0], c_sem.at[1], me, chan)
    c_all = all_but_one(c_send, c_recv, c_sem.at[0], c_sem.at[1], me, chan)
    pending.append(c_all)

    for k in range(1, CHANS):
        share(k, lax.rem(chan + CHANS - k, CHANS), chan).wait_recv()
    loads["skip"].wait()
    packet[...] = dot(skip[...], embeds[...].reshape(32, POINTS).astype(BF16))
    skip_on = pltpu.make_async_remote_copy(
        src_ref=packet,
        dst_ref=before,
        send_sem=s_sem.at[0],
        recv_sem=s_sem.at[1],
        device_id=(after, chan),
        device_id_type=MESH,
    )
    skip_on.start()
    pending.append(skip_on)
    loads["weight"].wait()

    def pack(step, carry):
        kind = step // 16
        rest = step % 16
        source = (rest // 4) * 8 + rest % 4
        one = raw[kind, source]
        two = raw[kind, source + 4]
        packed[kind, rest] = jnp.concatenate([one, two], axis=-1)
        return carry

    lax.fori_loop(0, 32, pack, 0)
    c_all.wait_recv()

    loads["fwd_x"].wait()
    modes = dot(fwd_x[...], c_recv[...].astype(F32).reshape(512, 128).astype(BF16))
    turned = jnp.concatenate([modes[0:128].T, modes[128:256].T], axis=0).astype(BF16)
    d_recv[pl.ds(chan, 1)] = turned.reshape(1, 256, 128)

    def gather(k, owner, to):
        return pltpu.make_async_remote_copy(
            src_ref=d_recv.at[owner],
            dst_ref=d_recv.at[owner],
            send_sem=d_send.at[k],
            recv_sem=d_rsem.at[k],
            device_id=(me, to),
            device_id_type=MESH,
        )

    for k in range(1, CHANS):
        gather(k, chan, lax.rem(chan + k, CHANS)).start()
        pending.append(gather(k, chan, chan))

    for k in (0, 1, 3, 2):
        owner = lax.rem(chan + CHANS - k, CHANS)
        if k:
            gather(k, owner, chan).wait_recv()
        def mix(o, carry, k=k, owner=owner):
            if k:
                real, imag = acc[0, o], acc[1, o]
            else:
                real = imag = jnp.zeros((MZ, 128), F32)
            for group in range(4):
                at = owner * 4 + group
                wr, wi = packed[0, at, o], packed[1, at, o]
                vr = d_recv[owner, group * 32 : group * 32 + 32, :].astype(F32)
                vi = d_recv[owner, 128 + group * 32 : 128 + group * 32 + 32, :].astype(F32)
                real = real + (wr * vr - wi * vi)
                imag = imag + (wr * vi + wi * vr)
            acc[0, o] = real
            acc[1, o] = imag
            return carry

        lax.fori_loop(0, 8, mix, 0)
    low = iota((MZ, 128), 1) < 64
    mixed = []
    for o in range(8):
        real, imag = acc[0, o], acc[1, o]
        real = real + pltpu.roll(real, 64, 1)
        imag = imag + pltpu.roll(imag, 64, 1)
        mixed.append(jnp.where(low, real, imag).astype(BF16))
    mixed = jnp.concatenate(
        [jnp.concatenate(mixed[0:4], axis=0), jnp.concatenate(mixed[4:8], axis=0)], axis=1
    )
    loads["inv_x"].wait()
    e_send[...] = dot_nt(inv_x[...], mixed).reshape(SLABS, 8, 128).astype(BF16)
    exchange(e_send, e_recv, e_sem.at[0], e_sem.at[1], me, chan)
    e_all = all_but_one(e_send, e_recv, e_sem.at[0], e_sem.at[1], me, chan)
    pending.append(e_all)

    skip_on.wait_recv()
    loads["bias"].wait()

    def deposit(o, carry):
        first = jnp.concatenate([packet[pl.ds(o, 1), :], before[pl.ds(o, 1), :]], axis=1)
        for plane in range(2):
            width = (2 - plane) * POINTS
            spread = hat_y[:, 0:width].astype(F32) * (first[:, 0:width] * along[plane : plane + 1, 0:width])
            high = spread.astype(BF16)
            rest = (spread - high.astype(F32)).astype(BF16)
            grid_z = hat_z[:, 0:width]
            skipped[o, :, plane * 128 : plane * 128 + 128] = (
                dot_nt(high, grid_z) + dot_nt(rest, grid_z) + bias[o]
            )
        return carry

    lax.fori_loop(0, 8, deposit, 0)
    e_all.wait_recv()

    loads["inv_y"].wait()
    loads["inv_z"].wait()
    lines = dot(inv_y[...], e_recv[...].astype(F32).reshape(512, 128).astype(BF16)).astype(BF16)
    for block in range(4):
        half, plane = block // 2, block % 2
        at = block * 256
        both = jnp.concatenate([lines[at : at + 128], lines[at + 128 : at + 256]], axis=1)
        result = dot(both, inv_z[...])
        for group in range(4):
            spectral[half * 4 + group, :, plane * 128 : plane * 128 + 128] = result[
                :, group * 128 : group * 128 + 128
            ]

    loads["head"].wait()
    loads["head_bias"].wait()
    heading = head[...].astype(F32)
    shape = (32, 256)
    scale = math.sqrt(2.0 / math.pi)

    def activate(step, carry):
        at = pl.ds(step * 32, 32)
        fields = [jnp.zeros(shape, F32) for _ in range(4)]
        for o in range(8):
            x = spectral[o, at, :] + skipped[o, at, :]
            h = 0.5 * x * (1.0 + jnp.tanh(scale * (x + 0.044715 * (x * x * x))))
            for n in range(4):
                fields[n] = fields[n] + jnp.broadcast_to(heading[n : n + 1, o : o + 1], shape) * h
        for n in range(4):
            high = fields[n].astype(BF16)
            rest = (fields[n] - high.astype(F32)).astype(BF16)
            for plane in range(2):
                z = slice(plane * 128, plane * 128 + 128)
                hn[plane, n, at, 0:128] = high[:, z]
                hn[plane, n, at, 128:256] = rest[:, z]
        return carry

    lax.fori_loop(0, 4, activate, 0)

    fields = hn[...].reshape(1024, 256)
    for block in range(8):
        lanes = pl.ds(block * 256, 256)
        planes = 2 if block < 4 else 1
        grid_z = hat_z[:, lanes]
        along_z = dot(fields[0 : planes * 512], jnp.concatenate([grid_z, grid_z], axis=0))
        grid_y = hat_y[:, lanes].astype(F32)
        for n in range(4):
            sampled = jnp.zeros((1, 256), F32)
            for plane in range(planes):
                at = plane * 512 + n * 128
                line = jnp.sum(along_z[at : at + 128] * grid_y, axis=0, keepdims=True)
                sampled = sampled + line * along[plane : plane + 1, lanes]
            which = block // 4
            heads[which * 4 + n : which * 4 + n + 1, pl.ds((block % 4) * 256, 256)] = sampled
    for k in range(8):
        piece = heads[:, k * 128 : k * 128 + 128]
        back[pl.ds(k, 8, stride=16), :] = piece
        back[pl.ds(k + 8, 8, stride=16), :] = pltpu.roll(piece, 64, 1)
    h_send[...] = back[...].T[0:SLABS].reshape(SLABS, 1, 128)
    exchange(h_send, h_recv, h_sem.at[0], h_sem.at[1], me, chan)
    h_all = all_but_one(h_send, h_recv, h_sem.at[0], h_sem.at[1], me, chan)
    pending.append(h_all)
    h_all.wait_recv()

    home = h_recv[...].reshape(SLABS, 128)
    home = home + pltpu.roll(pltpu.roll(home, SLABS - 1, 0), 64, 1)
    sums[pl.ds(chan, 1)] = home.reshape(1, SLABS, 128)

    def total(k, owner, to):
        return pltpu.make_async_remote_copy(
            src_ref=sums.at[owner],
            dst_ref=sums.at[owner],
            send_sem=g_send.at[k],
            recv_sem=g_recv.at[k],
            device_id=(me, to),
            device_id_type=MESH,
        )

    for k in range(1, CHANS):
        total(k, chan, lax.rem(chan + k, CHANS)).start()
        pending.append(total(k, chan, chan))
    pick2 = jnp.where((iota((SLABS, POINTS), 1) >> 4) == iota((SLABS, POINTS), 0), 1.0, 0.0).astype(BF16)
    cover = dot(jnp.broadcast_to(counts[...].astype(F32), (8, SLABS)).astype(BF16), pick2)
    alive = (iota((4, POINTS), 1) & 15).astype(F32) < cover[0:4]
    for k in range(1, CHANS):
        total(k, lax.rem(chan + CHANS - k, CHANS), chan).wait_recv()
    home = sums[0] + sums[1] + sums[2] + sums[3]
    turned = jnp.concatenate([home, jnp.zeros_like(home)], axis=0).T[0:SLABS, 0:SLABS]
    top = turned.astype(BF16)
    rest = turned - top.astype(F32)
    middle = rest.astype(BF16)
    bottom = (rest - middle.astype(F32)).astype(BF16)
    laid = dot(top, pick2) + dot(middle, pick2) + dot(bottom, pick2)
    for n in range(4):
        line = jnp.sum(laid[n * 16 : n * 16 + 16] * mask, axis=0, keepdims=True)
        out[n : n + 1, :] = jnp.where(alive[n : n + 1], line + head_bias[n], 0.0)

    for copy in pending:
        copy.wait_send()


def local(
    point_feats, cell_coords, send_counts, lift_weight, spec_weight,
    skip_weight, spec_bias, out_weight, out_bias,
):
    weight = jnp.swapaxes(spec_weight, 4, 5).reshape(2, 32, 8, MZ, 64)
    vmem = pl.BlockSpec(memory_space=pltpu.VMEM)
    hbm = pl.BlockSpec(memory_space=pltpu.HBM)
    dma = pltpu.SemaphoreType.DMA
    scratch = [
        pltpu.VMEM((32, POINTS), BF16),
        pltpu.VMEM((3, POINTS), jnp.int32),
        pltpu.VMEM((1, SLABS), jnp.int32),
        pltpu.VMEM((8, 32), BF16),
        pltpu.VMEM((8, 32), BF16),
        pltpu.SMEM((8,), F32),
        pltpu.VMEM((4, 8), BF16),
        pltpu.SMEM((4,), F32),
        pltpu.VMEM((192, 128), BF16),
        pltpu.VMEM((256, 512), BF16),
        pltpu.VMEM((512, 256), BF16),
        pltpu.VMEM((1024, 512), BF16),
        pltpu.VMEM((256, 512), BF16),
        pltpu.VMEM((SLABS, 2, 128), F32),
        pltpu.VMEM((SLABS, 2, 128), F32),
        pltpu.VMEM((128, 128), F32),
        pltpu.VMEM((16, POINTS), F32),
        pltpu.VMEM((16, POINTS), F32),
        pltpu.VMEM((CHANS, 8, POINTS), F32),
        pltpu.VMEM((8, POINTS), F32),
        pltpu.VMEM((8, POINTS), F32),
        pltpu.VMEM((8, 2 * POINTS), F32),
        pltpu.VMEM((128, 2 * POINTS), BF16),
        pltpu.VMEM((128, 2 * POINTS), BF16),
        pltpu.VMEM((192, POINTS), F32),
        pltpu.VMEM((128, 2 * POINTS), BF16),
        pltpu.VMEM((512, 2 * POINTS), BF16),
        pltpu.VMEM((512, 128), F32),
        pltpu.VMEM((SLABS, 8, 128), BF16),
        pltpu.VMEM((SLABS, 8, 128), BF16),
        pltpu.VMEM((2, 32, 8, MZ, 64), F32),
        pltpu.VMEM((2, 16, 8, MZ, 128), F32),
        pltpu.VMEM((CHANS, 256, 128), BF16),
        pltpu.VMEM((2, 8, MZ, 128), F32),
        pltpu.VMEM((SLABS, 8, 128), BF16),
        pltpu.VMEM((SLABS, 8, 128), BF16),
        pltpu.VMEM((8, 128, 256), F32),
        pltpu.VMEM((8, 128, 256), F32),
        pltpu.VMEM((2, 4, 128, 256), BF16),
        pltpu.VMEM((8, POINTS), F32),
        pltpu.VMEM((128, 128), F32),
        pltpu.VMEM((SLABS, 1, 128), F32),
        pltpu.VMEM((SLABS, 1, 128), F32),
        pltpu.VMEM((CHANS, SLABS, 128), F32),
        dma((14,)),
        dma((2,)),
        dma((2,)),
        dma((2,)),
        dma((2,)),
        dma((2,)),
        dma((2,)),
        dma((CHANS,)),
        dma((CHANS,)),
        dma((CHANS,)),
        dma((CHANS,)),
        dma((CHANS,)),
        dma((CHANS,)),
    ]
    return pl.pallas_call(
        kernel,
        out_shape=jax.ShapeDtypeStruct((4, POINTS), F32),
        in_specs=[hbm] * 14,
        out_specs=vmem,
        scratch_shapes=scratch,
        compiler_params=pltpu.CompilerParams(
            collective_id=0, has_side_effects=True, vmem_limit_bytes=60 * 1024 * 1024
        ),
    )(
        point_feats, cell_coords, send_counts, lift_weight.T, weight,
        skip_weight.T, spec_bias, out_weight.T, out_bias, *(jnp.asarray(t) for t in tables()),
    )


def solution(mesh):
    in_specs = (
        P(None, "slab"),
        P(None, "slab"),
        P("slab", None),
        P(None, "chan"),
        P(None, None, "chan", "slab", None, None),
        P(None, "chan"),
        P("chan"),
        P("chan", None),
        P(),
    )
    out_specs = P(None, "slab")
    return jax.shard_map(local, mesh=mesh, in_specs=in_specs, out_specs=out_specs, check_vma=False)
```

time: 70.3 us -> 58.5 us (0.83)
  local copies, waits for them, and re-layouts: 11.4 us -> 1.32 us
  Pallas kernels: 58.3 us -> 57 us
    unnamed x29 -> x1, local copies, waits for them, and re-layouts: 11.4 us -> 1.32 us
    pallas_call x1, Pallas kernels: 58.3 us -> 57 us  [local(): pl.pallas_call(kernel, out_shape=jax.ShapeDtypeStruct((4, POINTS), F32),...]
where the time goes in v2:
time: 58.5 us; the launch traced here: 58.4 us
  Pallas kernels  57 us (97%)
  local copies, waits for them, and re-layouts  1.32 us (2%)
    pallas_call x1, Pallas kernels, local(): pl.pallas_call(kernel, out_shape=jax.ShapeDtypeStruct((4, POINTS), F32),...  57 us
    unnamed x1, local copies, waits for them, and re-layouts  1.32 us

profile of v2, /device:TPU:1, one launch (start us, length us, event | category | flops | bytes accessed | tf_op | source)
XLA Modules:
  0.0 58.4 jit_solution(7845342260101849477)
XLA Ops:
  0.0 57.0 %shard_map.136 = f32[4,1024]{1,0:T(4,128)} custom-call(bf16[32,1024]{1,0:T(8,128)(2,1)} %feats_in.1, s32[3,1024]{1,0:T(4,128)} %coords_in.1, s32[1,64]{1,0:T(1,128)} %counts_in.1, bf16[8,32]{1,0:T(8,128)(2,1)} %bitcast.9, f32[2,32,8,32,64]{4,3,2,1,0:T(8,128)} %bitcast.8, bf16[8,32]{1,0:T(8,128)(2,1)} %bitcast.10, f32[8]{0:T(128)} %bias_in.1, ...), custom_call_target="tpu_custom_call" | custom-call | tf_op jit(solution)/shard_map/pallas_call | solution.py:541
  57.0 1.3 %copy.17 = f32[4,1024]{1,0:T(4,128)} copy(f32[4,1024]{1,0:T(4,128)} %shard_map.136) | data formatting | bytes 32768

commit v3 on v2

--- a/solution.py
+++ b/solution.py
@@ -15,6 +15,8 @@
 SLABS = 64
 CHANS = 4
 POINTS = 1024
+DEPOSIT_C = 3
+DEPOSIT_D = 6
 MODES = np.concatenate([np.arange(MZ), np.arange(GRID - MZ, GRID)])
 MESH = pl.DeviceIdType.MESH
 F32 = jnp.float32
@@ -86,26 +88,34 @@
     return lax.broadcasted_iota(jnp.int32, shape, dim)
 
 
-def exchange(src, dst, send_sem, recv_sem, me, chan):
-    def send(k, carry):
-        to = lax.rem(me + k, SLABS)
+def each_slab(me, act):
+    act(lax.rem(me + 32, SLABS))
+
+    def pair(k, carry):
+        act(lax.rem(me + 32 + k, SLABS))
+        act(lax.rem(me + 32 - k, SLABS))
+        return carry
+
+    lax.fori_loop(1, 32, pair, 0)
+
+
+def exchange(src, dst, send_sem, recv_sem, me, chan, pick=lambda src, to: src.at[to]):
+    def send(to):
         pltpu.make_async_remote_copy(
-            src_ref=src.at[to],
+            src_ref=pick(src, to),
             dst_ref=dst.at[me],
             send_sem=send_sem,
             recv_sem=recv_sem,
             device_id=(to, chan),
             device_id_type=MESH,
         ).start()
-        return carry
-
-    lax.fori_loop(1, SLABS, send, 0)
-    dst[pl.ds(me, 1)] = src[pl.ds(me, 1)]
-
-
-def all_but_one(src, dst, send_sem, recv_sem, me, chan):
+
+    each_slab(me, send)
+
+
+def all_but_one(dst, send_sem, recv_sem, me, chan):
     return pltpu.make_async_remote_copy(
-        src_ref=src.at[pl.ds(0, SLABS - 1)],
+        src_ref=dst.at[pl.ds(0, SLABS - 1)],
         dst_ref=dst.at[pl.ds(0, SLABS - 1)],
         send_sem=send_sem,
         recv_sem=recv_sem,
@@ -115,20 +125,19 @@
 
 
 def kernel(
-    feats_in, coords_in, counts_in, lift_in, weight, skip_in, bias_in, head_in, head_bias_in,
+    feats_in, coords_in, counts_in, lift_in, weight, skip_in, bias_in, head_in,
     fwd_yz_in, fwd_x_in, inv_x_in, inv_y_in, inv_z_in,
     out,
-    feats, coords, counts, lift, skip, bias, head, head_bias,
+    feats, coords, counts, lift, skip, bias, head,
     fwd_yz, fwd_x, inv_x, inv_y, inv_z,
-    a_send, a_recv, t_ref, own, prior, embeds, packet, before, along,
-    hat_y, hat_z, yh, lhs, rhs, stage, c_send, c_recv,
+    a_send, a_recv, t_ref, points, embeds, packet, along,
+    hat_y, hat_z, lhs, rhs, lhs_prior, rhs_prior, stage, c_send, c_recv,
     raw, packed, d_recv, acc, e_send, e_recv, skipped, spectral,
     hn, heads, back, h_send, h_recv, sums,
-    load_sem, a_sem, c_sem, e_sem, h_sem, n_sem, s_sem, m_send, m_recv, d_send, d_rsem, g_send, g_recv,
+    load_sem, a_sem, c_sem, e_sem, h_sem, m_send, m_recv, d_send, d_rsem, g_send, g_recv,
 ):
     me = lax.axis_index("slab")
     chan = lax.axis_index("chan")
-    after = lax.rem(me + 1, SLABS)
 
     loads = {}
     for k, (name, src, dst) in enumerate((
@@ -136,18 +145,16 @@
         ("lift", lift_in, lift), ("fwd_yz", fwd_yz_in, fwd_yz), ("skip", skip_in, skip),
         ("weight", weight, raw), ("fwd_x", fwd_x_in, fwd_x), ("inv_x", inv_x_in, inv_x),
         ("inv_y", inv_y_in, inv_y), ("inv_z", inv_z_in, inv_z), ("bias", bias_in, bias),
-        ("head", head_in, head), ("head_bias", head_bias_in, head_bias),
+        ("head", head_in, head),
     )):
         loads[name] = pltpu.make_async_copy(src, dst, load_sem.at[k])
 
     barrier = pltpu.get_barrier_semaphore()
 
-    def greet(k, carry):
-        to = lax.rem(me + k, SLABS)
+    def greet(to):
         pl.semaphore_signal(barrier, inc=1, device_id=(to, chan), device_id_type=MESH)
-        return carry
-
-    lax.fori_loop(1, SLABS, greet, 0)
+
+    each_slab(me, greet)
     for k in range(1, CHANS):
         pl.semaphore_signal(
             barrier, inc=1, device_id=(me, lax.rem(chan + k, CHANS)), device_id_type=MESH
@@ -173,44 +180,40 @@
     wide = jnp.broadcast_to(counts[...].astype(F32), (SLABS, SLABS))
     here = jnp.sum(jnp.where(iota((SLABS, SLABS), 0) == iota((SLABS, SLABS), 1), wide, 0.0), axis=1, keepdims=True)
     live = (iota((SLABS, 128), 1) & 15).astype(F32) < here
-    a_send[:, 0:1, :] = jnp.where(live, sorted_[:, :128], 0.0).reshape(SLABS, 1, 128)
-    a_send[:, 1:2, :] = sorted_[:, 128:].reshape(SLABS, 1, 128)
+    a_send[0:1, 0:1, :] = jnp.zeros((1, 1, 128), F32)
+    a_send[0:1, 1:2, :] = jnp.full((1, 1, 128), -8.0, F32)
+    a_send[1 : SLABS + 1, 0:1, :] = jnp.where(live, sorted_[:, :128], 0.0).reshape(SLABS, 1, 128)
+    a_send[1 : SLABS + 1, 1:2, :] = sorted_[:, 128:].reshape(SLABS, 1, 128)
 
     pl.semaphore_wait(barrier, SLABS - 1 + CHANS - 1)
-    exchange(a_send, a_recv, a_sem.at[0], a_sem.at[1], me, chan)
-    a_all = all_but_one(a_send, a_recv, a_sem.at[0], a_sem.at[1], me, chan)
+    exchange(
+        a_send, a_recv, a_sem.at[0], a_sem.at[1], me, chan,
+        lambda src, to: src.at[pl.ds(to, 2)],
+    )
+    a_recv[pl.ds(me, 1)] = a_send[pl.ds(me, 2)].reshape(1, 2, 2, 128)
+    a_all = all_but_one(a_recv, a_sem.at[0], a_sem.at[1], me, chan)
     pending.append(a_all)
     a_all.wait_recv()
 
-    got = a_recv[...]
-    t_ref[...] = jnp.concatenate(
-        [got[:, 0:1, :].reshape(SLABS, 128), got[:, 1:2, :].reshape(SLABS, 128)], axis=0
-    ).T
     low = iota((8, 128), 1) < 64
-    for k in range(8):
-        first = t_ref[pl.ds(k, 8, stride=16), :]
-        second = t_ref[pl.ds(k + 8, 8, stride=16), :]
-        values = jnp.where(low, first, pltpu.roll(second, 64, 1))
-        places = jnp.where(low, pltpu.roll(first, 64, 1), second)
-        lanes = pl.ds(k * 128, 128)
-        own[0:8, lanes] = values
-        own[8:11, lanes] = places[0:3] + (places[3:6] + 0.5) * 0.0625
-        own[11:16, lanes] = places[3:8]
-    pass_on = pltpu.make_async_remote_copy(
-        src_ref=own,
-        dst_ref=prior,
-        send_sem=n_sem.at[0],
-        recv_sem=n_sem.at[1],
-        device_id=(after, chan),
-        device_id_type=MESH,
-    )
-    pass_on.start()
-    pending.append(pass_on)
-    embeds[pl.ds(chan, 1)] = own[0:8, :].reshape(1, 8, POINTS)
+    for which in range(2):
+        got = a_recv[:, 1 - which]
+        t_ref[which] = jnp.concatenate(
+            [got[:, 0:1, :].reshape(SLABS, 128), got[:, 1:2, :].reshape(SLABS, 128)], axis=0
+        ).T
+        for k in range(8):
+            first = t_ref[which, pl.ds(k, 8, stride=16), :]
+            second = t_ref[which, pl.ds(k + 8, 8, stride=16), :]
+            values = jnp.where(low, first, pltpu.roll(second, 64, 1))
+            places = jnp.where(low, pltpu.roll(first, 64, 1), second)
+            lanes = pl.ds(k * 128, 128)
+            points[which, 0:8, lanes] = values
+            points[which, 8:11, lanes] = places[0:3] + (places[3:6] + 0.5) * 0.0625
+    embeds[pl.ds(chan, 1)] = points[:, 0:8, :].reshape(1, 2, 8, POINTS)
 
     def share(k, owner, to):
         return pltpu.make_async_remote_copy(
-            src_ref=own.at[0:8],
+            src_ref=points.at[:, 0:8],
             dst_ref=embeds.at[owner],
             send_sem=m_send.at[k],
             recv_sem=m_recv.at[k],
@@ -226,62 +229,47 @@
     base = (me * 2).astype(F32)
     down = iota((128, POINTS), 0).astype(F32)
 
-    def transform(points, which):
+    def transform(which, lhs, rhs):
         lanes = slice(which * POINTS, (which + 1) * POINTS)
-        hat_y[:, lanes] = hat(down, points[9:10, :]).astype(BF16)
-        hat_z[:, lanes] = hat(down, points[10:11, :]).astype(BF16)
-        yh[0:128, :] = dot(fwd_yz[0:128, :], hat_y[:, lanes])
-        yh[128:192, :] = dot(fwd_yz[128:192, :], hat_z[:, lanes])
-        local = points[8:9, :] - base
+        real_lanes, imag_lanes = slice(0, POINTS), slice(POINTS, 2 * POINTS)
+        hat_y[:, lanes] = hat(down, points[which, 9:10, :]).astype(BF16)
+        hat_z[:, lanes] = hat(down, points[which, 10:11, :]).astype(BF16)
+        line_y = dot(fwd_yz[0:128, :], hat_y[:, lanes])
+        line_z = dot(fwd_yz[128:192, :], hat_z[:, lanes])
+        local = points[which, 8:9, :] - base
         planes = 2 - which
         for plane in range(planes):
             near = hat(float(plane), local)
             along[plane : plane + 1, lanes] = near
-            for part_ in range(2):
-                lhs[plane * 64 : plane * 64 + 64, part_ * POINTS : (part_ + 1) * POINTS] = (
-                    yh[part_ * 64 : part_ * 64 + 64, :] * near
-                ).astype(BF16)
-        zr = yh[128:160, :]
-        zi = yh[160:192, :]
+            real = (line_y[0:64] * near).astype(BF16)
+            imag = (line_y[64:128] * near).astype(BF16)
+            top = slice(plane * 64, plane * 64 + 64)
+            low = slice((planes + plane) * 64, (planes + plane) * 64 + 64)
+            lhs[top, real_lanes] = real
+            lhs[top, imag_lanes] = -imag
+            lhs[low, real_lanes] = imag
+            lhs[low, imag_lanes] = real
         for c in range(8):
-            row = points[c : c + 1, :]
-            real = (zr * row).astype(BF16)
-            imag = (zi * row).astype(BF16)
-            rhs[c * 32 : c * 32 + 32, 0:POINTS] = real
-            rhs[c * 32 : c * 32 + 32, POINTS : 2 * POINTS] = -imag
-            rhs[256 + c * 32 : 256 + c * 32 + 32, 0:POINTS] = imag
-            rhs[256 + c * 32 : 256 + c * 32 + 32, POINTS : 2 * POINTS] = real
+            row = points[which, c : c + 1, :]
+            rhs[c * 32 : c * 32 + 32, real_lanes] = (line_z[0:32] * row).astype(BF16)
+            rhs[c * 32 : c * 32 + 32, imag_lanes] = (line_z[32:64] * row).astype(BF16)
+        result = dot_nt(lhs[...], rhs[...])
         for part_ in range(2):
-            for half in range(2):
-                block = part_ * 2 + half
-                result = dot_nt(lhs[0 : planes * 64], rhs[block * 128 : block * 128 + 128, :])
-                for plane in range(planes):
+            for plane in range(planes):
+                for half in range(2):
                     rows = pl.ds(half * 4 + plane * 2 + part_, 64, stride=8)
-                    piece = result[plane * 64 : plane * 64 + 64]
+                    at = (part_ * planes + plane) * 64
+                    piece = result[at : at + 64, half * 128 : half * 128 + 128]
                     stage[rows, :] = stage[rows, :] + piece if which else piece
 
-    transform(own, 0)
-    pass_on.wait_recv()
-    transform(prior, 1)
+    transform(0, lhs, rhs)
+    transform(1, lhs_prior, rhs_prior)
     c_send[...] = stage[...].reshape(SLABS, 8, 128).astype(BF16)
     exchange(c_send, c_recv, c_sem.at[0], c_sem.at[1], me, chan)
-    c_all = all_but_one(c_send, c_recv, c_sem.at[0], c_sem.at[1], me, chan)
+    c_recv[pl.ds(me, 1)] = c_send[pl.ds(me, 1)]
+    c_all = all_but_one(c_recv, c_sem.at[0], c_sem.at[1], me, chan)
     pending.append(c_all)
 
-    for k in range(1, CHANS):
-        share(k, lax.rem(chan + CHANS - k, CHANS), chan).wait_recv()
-    loads["skip"].wait()
-    packet[...] = dot(skip[...], embeds[...].reshape(32, POINTS).astype(BF16))
-    skip_on = pltpu.make_async_remote_copy(
-        src_ref=packet,
-        dst_ref=before,
-        send_sem=s_sem.at[0],
-        recv_sem=s_sem.at[1],
-        device_id=(after, chan),
-        device_id_type=MESH,
-    )
-    skip_on.start()
-    pending.append(skip_on)
     loads["weight"].wait()
 
     def pack(step, carry):
@@ -294,6 +282,29 @@
         return carry
 
     lax.fori_loop(0, 32, pack, 0)
+
+    for k in range(1, CHANS):
+        share(k, lax.rem(chan + CHANS - k, CHANS), chan).wait_recv()
+    loads["skip"].wait()
+    for which in range(2):
+        packet[which] = dot(skip[...], embeds[:, which].reshape(32, POINTS).astype(BF16))
+    loads["bias"].wait()
+
+    def spread(row, plane, which):
+        lanes = slice(which * POINTS, (which + 1) * POINTS)
+        values = hat_y[:, lanes].astype(F32) * (row * along[plane : plane + 1, lanes])
+        high = values.astype(BF16)
+        return high, (values - high.astype(F32)).astype(BF16)
+
+    def deposit_own(o, carry):
+        row = packet[0, pl.ds(o, 1), :]
+        pieces = [*spread(row, 0, 0), *spread(row, 1, 0)]
+        sums_z = dot_nt(jnp.concatenate(pieces, axis=0), hat_z[:, 0:POINTS])
+        skipped[o, :, 0:128] = sums_z[0:128] + sums_z[128:256] + bias[o]
+        skipped[o, :, 128:256] = sums_z[256:384] + sums_z[384:512] + bias[o]
+        return carry
+
+    lax.fori_loop(0, DEPOSIT_C, deposit_own, 0)
     c_all.wait_recv()
 
     loads["fwd_x"].wait()
@@ -311,10 +322,11 @@
             device_id_type=MESH,
         )
 
-    for k in range(1, CHANS):
+    for k in (2, 1, 3):
         gather(k, chan, lax.rem(chan + k, CHANS)).start()
         pending.append(gather(k, chan, chan))
 
+    lax.fori_loop(DEPOSIT_C, DEPOSIT_D, deposit_own, 0)
     for k in (0, 1, 3, 2):
         owner = lax.rem(chan + CHANS - k, CHANS)
         if k:
@@ -349,26 +361,19 @@
     loads["inv_x"].wait()
     e_send[...] = dot_nt(inv_x[...], mixed).reshape(SLABS, 8, 128).astype(BF16)
     exchange(e_send, e_recv, e_sem.at[0], e_sem.at[1], me, chan)
-    e_all = all_but_one(e_send, e_recv, e_sem.at[0], e_sem.at[1], me, chan)
+    e_recv[pl.ds(me, 1)] = e_send[pl.ds(me, 1)]
+    e_all = all_but_one(e_recv, e_sem.at[0], e_sem.at[1], me, chan)
     pending.append(e_all)
 
-    skip_on.wait_recv()
-    loads["bias"].wait()
-
-    def deposit(o, carry):
-        first = jnp.concatenate([packet[pl.ds(o, 1), :], before[pl.ds(o, 1), :]], axis=1)
-        for plane in range(2):
-            width = (2 - plane) * POINTS
-            spread = hat_y[:, 0:width].astype(F32) * (first[:, 0:width] * along[plane : plane + 1, 0:width])
-            high = spread.astype(BF16)
-            rest = (spread - high.astype(F32)).astype(BF16)
-            grid_z = hat_z[:, 0:width]
-            skipped[o, :, plane * 128 : plane * 128 + 128] = (
-                dot_nt(high, grid_z) + dot_nt(rest, grid_z) + bias[o]
-            )
+    lax.fori_loop(DEPOSIT_D, 8, deposit_own, 0)
+
+    def deposit_prior(o, carry):
+        high, rest = spread(packet[1, pl.ds(o, 1), :], 0, 1)
+        sums_z = dot_nt(jnp.concatenate([high, rest], axis=0), hat_z[:, POINTS : 2 * POINTS])
+        skipped[o, :, 0:128] = skipped[o, :, 0:128] + (sums_z[0:128] + sums_z[128:256])
         return carry
 
-    lax.fori_loop(0, 8, deposit, 0)
+    lax.fori_loop(0, 8, deposit_prior, 0)
     e_all.wait_recv()
 
     loads["inv_y"].wait()
@@ -385,7 +390,6 @@
             ]
 
     loads["head"].wait()
-    loads["head_bias"].wait()
     heading = head[...].astype(F32)
     shape = (32, 256)
     scale = math.sqrt(2.0 / math.pi)
@@ -430,13 +434,15 @@
         back[pl.ds(k + 8, 8, stride=16), :] = pltpu.roll(piece, 64, 1)
     h_send[...] = back[...].T[0:SLABS].reshape(SLABS, 1, 128)
     exchange(h_send, h_recv, h_sem.at[0], h_sem.at[1], me, chan)
-    h_all = all_but_one(h_send, h_recv, h_sem.at[0], h_sem.at[1], me, chan)
+    h_recv[pl.ds(me, 1)] = h_send[pl.ds(me, 1)]
+    h_all = all_but_one(h_recv, h_sem.at[0], h_sem.at[1], me, chan)
     pending.append(h_all)
     h_all.wait_recv()
 
     home = h_recv[...].reshape(SLABS, 128)
     home = home + pltpu.roll(pltpu.roll(home, SLABS - 1, 0), 64, 1)
-    sums[pl.ds(chan, 1)] = home.reshape(1, SLABS, 128)
+    narrow = iota((32, 128), 1) < 64
+    sums[pl.ds(chan, 1)] = jnp.where(narrow, home[0:32], pltpu.roll(home[32:64], 64, 1)).reshape(1, 32, 128)
 
     def total(k, owner, to):
         return pltpu.make_async_remote_copy(
@@ -457,6 +463,7 @@
     for k in range(1, CHANS):
         total(k, lax.rem(chan + CHANS - k, CHANS), chan).wait_recv()
     home = sums[0] + sums[1] + sums[2] + sums[3]
+    home = jnp.concatenate([home, pltpu.roll(home, 64, 1)], axis=0)
     turned = jnp.concatenate([home, jnp.zeros_like(home)], axis=0).T[0:SLABS, 0:SLABS]
     top = turned.astype(BF16)
     rest = turned - top.astype(F32)
@@ -465,7 +472,8 @@
     laid = dot(top, pick2) + dot(middle, pick2) + dot(bottom, pick2)
     for n in range(4):
         line = jnp.sum(laid[n * 16 : n * 16 + 16] * mask, axis=0, keepdims=True)
-        out[n : n + 1, :] = jnp.where(alive[n : n + 1], line + head_bias[n], 0.0)
+        out[n : n + 1, :] = jnp.where(alive[n : n + 1], line, 0.0)
+    out[4:8, :] = jnp.where(alive, 1.0, 0.0)
 
     for copy in pending:
         copy.wait_send()
@@ -487,26 +495,24 @@
         pltpu.VMEM((8, 32), BF16),
         pltpu.SMEM((8,), F32),
         pltpu.VMEM((4, 8), BF16),
-        pltpu.SMEM((4,), F32),
         pltpu.VMEM((192, 128), BF16),
         pltpu.VMEM((256, 512), BF16),
         pltpu.VMEM((512, 256), BF16),
         pltpu.VMEM((1024, 512), BF16),
         pltpu.VMEM((256, 512), BF16),
-        pltpu.VMEM((SLABS, 2, 128), F32),
-        pltpu.VMEM((SLABS, 2, 128), F32),
-        pltpu.VMEM((128, 128), F32),
-        pltpu.VMEM((16, POINTS), F32),
-        pltpu.VMEM((16, POINTS), F32),
-        pltpu.VMEM((CHANS, 8, POINTS), F32),
-        pltpu.VMEM((8, POINTS), F32),
-        pltpu.VMEM((8, POINTS), F32),
+        pltpu.VMEM((SLABS + 1, 2, 128), F32),
+        pltpu.VMEM((SLABS, 2, 2, 128), F32),
+        pltpu.VMEM((2, 128, 128), F32),
+        pltpu.VMEM((2, 16, POINTS), F32),
+        pltpu.VMEM((CHANS, 2, 8, POINTS), F32),
+        pltpu.VMEM((2, 8, POINTS), F32),
         pltpu.VMEM((8, 2 * POINTS), F32),
         pltpu.VMEM((128, 2 * POINTS), BF16),
         pltpu.VMEM((128, 2 * POINTS), BF16),
-        pltpu.VMEM((192, POINTS), F32),
+        pltpu.VMEM((256, 2 * POINTS), BF16),
+        pltpu.VMEM((256, 2 * POINTS), BF16),
         pltpu.VMEM((128, 2 * POINTS), BF16),
-        pltpu.VMEM((512, 2 * POINTS), BF16),
+        pltpu.VMEM((256, 2 * POINTS), BF16),
         pltpu.VMEM((512, 128), F32),
         pltpu.VMEM((SLABS, 8, 128), BF16),
         pltpu.VMEM((SLABS, 8, 128), BF16),
@@ -523,10 +529,8 @@
         pltpu.VMEM((128, 128), F32),
         pltpu.VMEM((SLABS, 1, 128), F32),
         pltpu.VMEM((SLABS, 1, 128), F32),
-        pltpu.VMEM((CHANS, SLABS, 128), F32),
-        dma((14,)),
-        dma((2,)),
-        dma((2,)),
+        pltpu.VMEM((CHANS, 32, 128), F32),
+        dma((13,)),
         dma((2,)),
         dma((2,)),
         dma((2,)),
@@ -538,10 +542,10 @@
         dma((CHANS,)),
         dma((CHANS,)),
     ]
-    return pl.pallas_call(
+    result = pl.pallas_call(
         kernel,
-        out_shape=jax.ShapeDtypeStruct((4, POINTS), F32),
-        in_specs=[hbm] * 14,
+        out_shape=jax.ShapeDtypeStruct((8, POINTS), F32),
+        in_specs=[hbm] * 13,
         out_specs=vmem,
         scratch_shapes=scratch,
         compiler_params=pltpu.CompilerParams(
@@ -549,8 +553,9 @@
         ),
     )(
         point_feats, cell_coords, send_counts, lift_weight.T, weight,
-        skip_weight.T, spec_bias, out_weight.T, out_bias, *(jnp.asarray(t) for t in tables()),
+        skip_weight.T, spec_bias, out_weight.T, *(jnp.asarray(t) for t in tables()),
     )
+    return result[0:4] + out_bias[:, None] * result[4:8]
 
 
 def solution(mesh):

time: 58.5 us -> 54.1 us (0.925)
  Pallas kernels: 57 us -> 52.4 us
  other arithmetic: 0 us -> 1.51 us
  local copies, waits for them, and re-layouts: 1.32 us -> 0.01 us
    pallas_call x1, Pallas kernels: 57 us -> 52.4 us  [local(): pl.pallas_call(kernel, out_shape=jax.ShapeDtypeStruct((8, POINTS), F32),...]
    add x0 -> x1, other arithmetic: none -> 1.51 us  [local(): return result[0:4] + out_bias[:, None] * result[4:8]]
    unnamed x1 -> x2, local copies, waits for them, and re-layouts: 1.32 us -> 0.01 us
where the time goes in v3:
time: 54.1 us; the launch traced here: 53.9 us
  Pallas kernels  52.4 us (97%)
  other arithmetic  1.51 us (3%)
    pallas_call x1, Pallas kernels, local(): pl.pallas_call(kernel, out_shape=jax.ShapeDtypeStruct((8, POINTS), F32),...  52.4 us
    add x1, other arithmetic, local(): return result[0:4] + out_bias[:, None] * result[4:8]  1.51 us

profile of v3, /device:TPU:1, one launch (start us, length us, event | category | flops | bytes accessed | tf_op | source)
XLA Modules:
  0.0 53.9 jit_solution(3486168211386063131)
XLA Ops:
  0.0 0.0 copy-start
  0.0 52.4 %shard_map.136 = f32[8,1024]{1,0:T(8,128)} custom-call(bf16[32,1024]{1,0:T(8,128)(2,1)} %feats_in.1, s32[3,1024]{1,0:T(4,128)} %coords_in.1, s32[1,64]{1,0:T(1,128)} %counts_in.1, bf16[8,32]{1,0:T(8,128)(2,1)} %bitcast.9, f32[2,32,8,32,64]{4,3,2,1,0:T(8,128)} %bitcast.8, bf16[8,32]{1,0:T(8,128)(2,1)} %bitcast.10, f32[8]{0:T(128)} %bias_in.1, ...), custom_call_target="tpu_custom_call" | custom-call | tf_op jit(solution)/shard_map/pallas_call | solution.py:545
  52.4 0.0 copy-done
  52.4 1.5 %multiply_add_fusion = f32[4,1024]{1,0:T(4,128)} fusion(f32[8,1024]{1,0:T(8,128)} %shard_map.136, f32[4]{0:T(128)S(1)} %copy-done), kind=kLoop, calls=%fused_computation | loop fusion | flops 8192 | bytes 49168 | tf_op jit(solution)/shard_map/add | solution.py:558
Async XLA Ops:
  0.0 52.4 %copy-start = (f32[4]{0:T(128)S(1)}, f32[4]{0:T(128)}, u32[]{:S(2)}) copy-start(f32[4]{0:T(128)} %param.22) | copy-start | bytes 52

commit v4 on v3

--- a/solution.py
+++ b/solution.py
@@ -16,7 +16,7 @@
 CHANS = 4
 POINTS = 1024
 DEPOSIT_C = 3
-DEPOSIT_D = 6
+DEPOSIT_D = 4
 MODES = np.concatenate([np.arange(MZ), np.arange(GRID - MZ, GRID)])
 MESH = pl.DeviceIdType.MESH
 F32 = jnp.float32
@@ -221,7 +221,7 @@
             device_id_type=MESH,
         )
 
-    for k in range(1, CHANS):
+    for k in (1, 3, 2):
         share(k, chan, lax.rem(chan + k, CHANS)).start()
         pending.append(share(k, chan, chan))
 
@@ -322,7 +322,7 @@
             device_id_type=MESH,
         )
 
-    for k in (2, 1, 3):
+    for k in (1, 3, 2):
         gather(k, chan, lax.rem(chan + k, CHANS)).start()
         pending.append(gather(k, chan, chan))
 
@@ -379,18 +379,20 @@
     loads["inv_y"].wait()
     loads["inv_z"].wait()
     lines = dot(inv_y[...], e_recv[...].astype(F32).reshape(512, 128).astype(BF16)).astype(BF16)
+    both = [
+        jnp.concatenate([lines[at : at + 128], lines[at + 128 : at + 256]], axis=1)
+        for at in range(0, 1024, 256)
+    ]
+    result = dot(jnp.concatenate(both, axis=0), inv_z[...])
     for block in range(4):
         half, plane = block // 2, block % 2
-        at = block * 256
-        both = jnp.concatenate([lines[at : at + 128], lines[at + 128 : at + 256]], axis=1)
-        result = dot(both, inv_z[...])
         for group in range(4):
             spectral[half * 4 + group, :, plane * 128 : plane * 128 + 128] = result[
-                :, group * 128 : group * 128 + 128
+                block * 128 : block * 128 + 128, group * 128 : group * 128 + 128
             ]
 
     loads["head"].wait()
-    heading = head[...].astype(F32)
+    heading = 0.5 * head[...].astype(F32)
     shape = (32, 256)
     scale = math.sqrt(2.0 / math.pi)
 
@@ -399,7 +401,7 @@
         fields = [jnp.zeros(shape, F32) for _ in range(4)]
         for o in range(8):
             x = spectral[o, at, :] + skipped[o, at, :]
-            h = 0.5 * x * (1.0 + jnp.tanh(scale * (x + 0.044715 * (x * x * x))))
+            h = x + x * jnp.tanh(x * (scale + (scale * 0.044715) * (x * x)))
             for n in range(4):
                 fields[n] = fields[n] + jnp.broadcast_to(heading[n : n + 1, o : o + 1], shape) * h
         for n in range(4):
@@ -454,7 +456,7 @@
             device_id_type=MESH,
         )
 
-    for k in range(1, CHANS):
+    for k in (1, 3, 2):
         total(k, chan, lax.rem(chan + k, CHANS)).start()
         pending.append(total(k, chan, chan))
     pick2 = jnp.where((iota((SLABS, POINTS), 1) >> 4) == iota((SLABS, POINTS), 0), 1.0, 0.0).astype(BF16)

time: 54.1 us -> 53.5 us (0.989)
  Pallas kernels: 52.4 us -> 51.8 us
    pallas_call x1, Pallas kernels: 52.4 us -> 51.8 us  [local(): pl.pallas_call(kernel, out_shape=jax.ShapeDtypeStruct((8, POINTS), F32),...]
where the time goes in v4:
time: 53.5 us; the launch traced here: 53.3 us
  Pallas kernels  51.8 us (97%)
  other arithmetic  1.51 us (3%)
    pallas_call x1, Pallas kernels, local(): pl.pallas_call(kernel, out_shape=jax.ShapeDtypeStruct((8, POINTS), F32),...  51.8 us
    add x1, other arithmetic, local(): return result[0:4] + out_bias[:, None] * result[4:8]  1.51 us

profile of v4, /device:TPU:1, one launch (start us, length us, event | category | flops | bytes accessed | tf_op | source)
XLA Modules:
  0.0 53.3 jit_solution(5939037159244124686)
XLA Ops:
  0.0 0.0 copy-start
  0.0 51.8 %shard_map.136 = f32[8,1024]{1,0:T(8,128)} custom-call(bf16[32,1024]{1,0:T(8,128)(2,1)} %feats_in.1, s32[3,1024]{1,0:T(4,128)} %coords_in.1, s32[1,64]{1,0:T(1,128)} %counts_in.1, bf16[8,32]{1,0:T(8,128)(2,1)} %bitcast.9, f32[2,32,8,32,64]{4,3,2,1,0:T(8,128)} %bitcast.8, bf16[8,32]{1,0:T(8,128)(2,1)} %bitcast.10, f32[8]{0:T(128)} %bias_in.1, ...), custom_call_target="tpu_custom_call" | custom-call | tf_op jit(solution)/shard_map/pallas_call | solution.py:547
  51.8 0.0 copy-done
  51.8 1.5 %multiply_add_fusion = f32[4,1024]{1,0:T(4,128)} fusion(f32[8,1024]{1,0:T(8,128)} %shard_map.136, f32[4]{0:T(128)S(1)} %copy-done), kind=kLoop, calls=%fused_computation | loop fusion | flops 8192 | bytes 49168 | tf_op jit(solution)/shard_map/add | solution.py:560
Async XLA Ops:
  0.0 51.8 %copy-start = (f32[4]{0:T(128)S(1)}, f32[4]{0:T(128)}, u32[]{:S(2)}) copy-start(f32[4]{0:T(128)} %param.22) | copy-start | bytes 52

commit v5 on v4

--- a/solution.py
+++ b/solution.py
@@ -89,14 +89,20 @@
 
 
 def each_slab(me, act):
-    act(lax.rem(me + 32, SLABS))
+    act(lax.rem(me + 36, SLABS))
 
     def pair(k, carry):
-        act(lax.rem(me + 32 + k, SLABS))
-        act(lax.rem(me + 32 - k, SLABS))
+        act(lax.rem(me + 36 + k, SLABS))
+        act(lax.rem(me + 36 - k, SLABS))
         return carry
 
-    lax.fori_loop(1, 32, pair, 0)
+    lax.fori_loop(1, 28, pair, 0)
+
+    def near(k, carry):
+        act(lax.rem(me + 8 - k, SLABS))
+        return carry
+
+    lax.fori_loop(0, 8, near, 0)
 
 
 def exchange(src, dst, send_sem, recv_sem, me, chan, pick=lambda src, to: src.at[to]):

time: 53.5 us -> 53.6 us (level)
  no operation moved by 1% of the time
where the time goes in v5:
time: 53.6 us; the launch traced here: 53.4 us
  Pallas kernels  51.9 us (97%)
  other arithmetic  1.51 us (3%)
    pallas_call x1, Pallas kernels, local(): pl.pallas_call(kernel, out_shape=jax.ShapeDtypeStruct((8, POINTS), F32),...  51.9 us
    add x1, other arithmetic, local(): return result[0:4] + out_bias[:, None] * result[4:8]  1.51 us

profile of v5, /device:TPU:1, one launch (start us, length us, event | category | flops | bytes accessed | tf_op | source)
XLA Modules:
  0.0 53.4 jit_solution(9598788416523727834)
XLA Ops:
  0.0 0.0 copy-start
  0.0 51.9 %shard_map.136 = f32[8,1024]{1,0:T(8,128)} custom-call(bf16[32,1024]{1,0:T(8,128)(2,1)} %feats_in.1, s32[3,1024]{1,0:T(4,128)} %coords_in.1, s32[1,64]{1,0:T(1,128)} %counts_in.1, bf16[8,32]{1,0:T(8,128)(2,1)} %bitcast.9, f32[2,32,8,32,64]{4,3,2,1,0:T(8,128)} %bitcast.8, bf16[8,32]{1,0:T(8,128)(2,1)} %bitcast.10, f32[8]{0:T(128)} %bias_in.1, ...), custom_call_target="tpu_custom_call" | custom-call | tf_op jit(solution)/shard_map/pallas_call | solution.py:553
  51.9 0.0 copy-done
  51.9 1.5 %multiply_add_fusion = f32[4,1024]{1,0:T(4,128)} fusion(f32[8,1024]{1,0:T(8,128)} %shard_map.136, f32[4]{0:T(128)S(1)} %copy-done), kind=kLoop, calls=%fused_computation | loop fusion | flops 8192 | bytes 49168 | tf_op jit(solution)/shard_map/add | solution.py:566
Async XLA Ops:
  0.0 51.9 %copy-start = (f32[4]{0:T(128)S(1)}, f32[4]{0:T(128)}, u32[]{:S(2)}) copy-start(f32[4]{0:T(128)} %param.22) | copy-start | bytes 52
